TPU v7x, 32 devices: a whole 2x2x4 slice. The times are simulated.
32 devices in a mesh: ctx: 8 (over z, y), tp: 4 (over x, core).
Axes of the slice: x: 2, y: 2, z: 4, core: 2. Of those that a mesh axis runs over, the one named last changes fastest.
Arguments:
- projected: bfloat16 [1024, 4, 4640], P('ctx', 'tp'), may hold values from -6 to 6
- conv_weight: float32 [4, 4, 2560], P('tp'), may hold values from -3 to 3
- conv_bias: float32 [4, 2560], P('tp'), may hold values from -1.5 to 1.5
- step_bias: float32 [4, 32], P('tp'), may hold values from -1 to 0.5
- log_rates: float32 [4, 32], P('tp'), as said below
- norm_gain: float32 [4, 2048], P('tp'), may hold values from 0.1 to 1.9
- out_weight: bfloat16 [4, 2048, 4096], P('tp', 'ctx'), may hold values from -0.0625 to 0.0625
Outputs:
- mixed: bfloat16 [1024, 4096], P('ctx', 'tp')
Inputs may be any that keep to these rules, and one draw needn't show every extreme that they name: log_rates lies between log(0.3 / 1024) and log(1 / 25).
All inputs are finite; a program needn't handle non-finite values.
Results may differ from a plain program's by a relative error of at most 0.0058.
Values may be sent and summed in bfloat16 or wider, within the bound.
A program may use at most 320 MiB of HBM per device.

v0:
```python
import jax
import jax.numpy as jnp
import numpy as np
from jax import lax
from jax.sharding import PartitionSpec as P

P_SIZE = 64
N = 256
KCONV = 4
SPAN = 128
GCH = 2048
GCONV = 2560


highest_precision = lax.Precision.HIGHEST


def from_behind(shard, axis, by):
    peers = lax.axis_size(axis)
    pairs = [(i, i + by) for i in range(peers) if 0 <= i + by < peers]
    return lax.ppermute(shard, axis, pairs)


def ssd_blocks(inputs_x, step_sizes, decay_rate, b_keys, c_keys, block_rows):
    row_count = inputs_x.shape[0]
    block_count = row_count // block_rows
    head_count = inputs_x.shape[1]
    head_width = inputs_x.shape[2]
    state_count = b_keys.shape[1]
    x_blocks = inputs_x.reshape(block_count, block_rows, head_count, head_width)
    step_blocks = step_sizes.reshape(block_count, block_rows, head_count)
    b_blocks = b_keys.reshape(block_count, block_rows, state_count)
    c_blocks = c_keys.reshape(block_count, block_rows, state_count)
    causal_mask = (jnp.arange(block_rows)[:, None] >= jnp.arange(block_rows)[None, :])[None]

    def advance(carried, pieces):
        x_block, step_block, b_block, c_block = pieces
        log_steps = step_block * decay_rate[None, :]
        running = jnp.cumsum(log_steps, axis=0)
        intersection = jnp.dot(c_block, b_block.T, preferred_element_type=jnp.float32)
        b_float = b_block.astype(jnp.float32)
        c_float = c_block.astype(jnp.float32)
        log_gaps = running.T[:, :, None] - running.T[:, None, :]
        factors = jnp.where(causal_mask, jnp.exp(jnp.where(causal_mask, log_gaps, 0.0)), 0.0)
        factors = factors * intersection[None] * step_block.T[:, None, :]
        within = jnp.einsum("hts,shp->thp", factors, x_block, precision=highest_precision)
        carried_part = (
            jnp.einsum("tn,hpn->thp", c_float, carried, precision=highest_precision)
            * jnp.exp(running)[:, :, None]
        )
        tail_weight = jnp.exp(running[-1][None, :] - running) * step_block
        weighted = x_block * tail_weight[:, :, None]
        updated = carried * jnp.exp(running[-1])[:, None, None] + jnp.einsum(
            "shp,sn->hpn", weighted, b_float, precision=highest_precision
        )
        return (updated, within + carried_part)

    initial = jnp.zeros((head_count, head_width, state_count), jnp.float32)
    final_state, outputs = lax.scan(advance, initial, (x_blocks, step_blocks, b_blocks, c_blocks))
    total_log = jnp.sum(step_sizes * decay_rate[None, :], axis=0)
    return (outputs.reshape(row_count, head_count, head_width), final_state, total_log)


def on_device(projected, conv_weight, conv_bias, step_bias, log_rates, norm_gain, out_weight):
    row_count = projected.shape[0]
    conv_input = projected[:, :, GCH : GCH + GCONV]
    rim_rows = from_behind(conv_input[row_count - (KCONV - 1) :], "ctx", 1)
    padded = jnp.concatenate([rim_rows, conv_input], axis=0).astype(jnp.float32)
    mixed_conv = conv_bias[None]
    for offset in range(KCONV):
        mixed_conv = mixed_conv + conv_weight[:, offset][None] * padded[offset : offset + row_count]
    activated = jax.nn.silu(mixed_conv).astype(jnp.bfloat16)
    values = activated[:, :, :GCH]
    key_rows = activated[:, :, GCH:]
    raw_steps = projected[:, :, GCH + GCONV :]
    decay_rate = -jnp.exp(log_rates)
    devices = lax.axis_size("ctx")
    shard_width = GCH // devices
    shard_heads = max(1, shard_width // P_SIZE)
    piece_width = shard_width // shard_heads
    head_table = (
        np.arange(devices)[:, None] * shard_width // P_SIZE + np.arange(shard_heads)[None, :]
    ).reshape(-1)
    spread_steps = jnp.take(raw_steps, jnp.asarray(head_table, jnp.int32), axis=2)
    local_values, local_steps = (
        lax.all_to_all(values, "ctx", split_axis=2, concat_axis=0, tiled=True),
        lax.all_to_all(spread_steps, "ctx", split_axis=2, concat_axis=0, tiled=True),
    )
    all_keys = lax.all_gather(key_rows, "ctx", axis=0, tiled=True)
    sequence = local_values.shape[0]
    first_head = lax.axis_index("ctx") * shard_width // P_SIZE
    bias_slice = lax.dynamic_slice_in_dim(step_bias[0], first_head, shard_heads)
    rate_slice = lax.dynamic_slice_in_dim(decay_rate[0], first_head, shard_heads)
    step_sizes = jax.nn.softplus(local_steps[:, 0].astype(jnp.float32) + bias_slice[None, :])
    outputs, final_state, total_log = ssd_blocks(
        local_values[:, 0].astype(jnp.float32).reshape(sequence, shard_heads, piece_width),
        step_sizes,
        rate_slice,
        all_keys[:, 0, :N],
        all_keys[:, 0, N:],
        4 * SPAN,
    )
    pieces_out = [outputs.reshape(sequence, shard_width).astype(jnp.bfloat16)]
    scanned = lax.all_to_all(
        jnp.stack(pieces_out, axis=1), "ctx", split_axis=0, concat_axis=2, tiled=True
    )
    gated = scanned.astype(jnp.float32) * jax.nn.silu(projected[:, :, :GCH].astype(jnp.float32))
    normed = (
        gated * lax.rsqrt(jnp.mean(gated * gated, axis=2, keepdims=True) + 1e-05) * norm_gain[None]
    ).astype(jnp.bfloat16)
    summed = jnp.einsum(
        "tgr,grd->td",
        normed,
        lax.all_gather(out_weight, "ctx", axis=1, tiled=True),
        preferred_element_type=jnp.float32,
    )
    shares = lax.psum_scatter(summed, "tp", scatter_dimension=1, tiled=True)
    return shares.astype(jnp.bfloat16)


def solution(mesh):
    return jax.shard_map(
        on_device,
        mesh=mesh,
        in_specs=(
            P("ctx", "tp", None),
            P("tp", None, None),
            P("tp", None),
            P("tp", None),
            P("tp", None),
            P("tp", None),
            P("tp", "ctx", None),
        ),
        out_specs=P("ctx", "tp"),
        check_vma=False,
    )
```

profile of v0, /device:TPU:0, one launch (start us, length us, event | category | flops | bytes accessed | tf_op | source)
XLA Modules:
  0.0 352.2 jit_solution(252141890222170652)
XLA Ops:
  6.5 1.3 slice.61
  7.9 0.3 copy.99
  8.2 4.9 %collective-permute-start = (bf16[3,1,2560]{2,0,1:T(4,128)(2,1)S(1)}, bf16[3,1,2560]{2,0,1:T(4,128)(2,1)S(1)}, u32[]{:S(2)}, u32[]{:S(2)}) collective-permute-start(bf16[3,1,2560]{2,0,1:T(4,128)(2,1)S(1)} %copy.99), channel_id=1, source_target_pairs={{0,4},{4,8},{8,12},{12,16},{16,20},{20,24},{24,28},{1,5},{5,9},{9,... | collective-permute-start | bytes 46088 | tf_op jit(solution)/shard_map/ppermute | solution.py:21
  13.1 0.1 slice_reduce_fusion.5
  13.2 0.3 copy.100
  13.5 0.4 copy-done.5
  13.9 0.6 collective-permute-done
  14.5 0.2 maximum_convert_fusion
  14.7 0.8 multiply_convert_fusion
  15.6 0.7 slice.90
  16.3 0.7 all-gather.5.cloned.1.call-update
  17.1 0.6 gather_fusion
  17.8 0.5 broadcast.101
  18.3 0.7 reduce.14
  19.0 0.6 reshape.229
  19.6 6.6 %all-to-all-start = ((bf16[8,2,256]{2,1,0:T(2,128)(2,1)}), bf16[8,2,256]{2,1,0:T(2,128)(2,1)S(1)}, u32[]{:S(2)}, u32[]{:S(2)}) async-start(bf16[8,2,256]{2,1,0:T(2,128)(2,1)} %reshape.229), calls=%async_computation | async-start | bytes 16384 | tf_op jit(solution)/shard_map/all_to_all | solution.py:87
  26.2 0.8 copy.89
  27.0 11.5 %reduce.15 = bf16[2048,128]{1,0:T(8,128)(2,1)S(1)} reduce(bf16[2048,1,128]{2,1,0:T(2,128)(2,1)S(1)} %bitcast.135, bf16[]{:T(256)} %broadcast.101), dimensions={1}, to_apply=%bitcast.89.reduce_sub_computation | reduce | bytes 1048578
  38.5 0.9 reshape.231
  39.5 6.0 %all-to-all-start.1 = ((bf16[8,2,16384]{2,1,0:T(2,128)(2,1)}), bf16[8,2,16384]{2,1,0:T(2,128)(2,1)S(1)}, u32[]{:S(2)}, u32[]{:S(2)}) async-start(bf16[8,2,16384]{2,1,0:T(2,128)(2,1)} %reshape.231), calls=%async_computation.1 | async-start | bytes 1048576 | tf_op jit(solution)/shard_map/all_to_all | solution.py:86
  45.5 0.2 reduce-scatter.2.cloned.1.call-start
  45.9 0.1 compare_select_fusion
  46.0 19.9 %all-to-all-done.1 = bf16[8,2,16384]{2,1,0:T(2,128)(2,1)S(1)} async-done(((bf16[8,2,16384]{2,1,0:T(2,128)(2,1)}), bf16[8,2,16384]{2,1,0:T(2,128)(2,1)S(1)}, u32[]{:S(2)}, u32[]{:S(2)}) %all-to-all-start.1) | async-done | bytes 524320 | tf_op jit(solution)/shard_map/all_to_all | solution.py:86
  66.0 0.5 reshape.232
  66.5 1.1 bitcast_convert_fusion
  67.6 0.6 copy.120
  68.3 0.5 reshape.202
  68.8 1.3 fusion.62
  70.1 19.8 %while.14 = (s32[]{:T(128)}, f32[4,64,256]{2,1,0:T(8,128)S(1)}, bf16[2,512,4,64]{1,3,2,0:T(8,128)(2,1)}, f32[2,512,4]{1,2,0:T(4,128)S(1)}, f32[4]{0:T(128)S(1)},...) while((s32[]{:T(128)}, f32[4,64,256]{2,1,0:T(8,128)S(1)}, ...), condition=%wide.region_3.4_spmd.clone.clone, body=%wide.region_0.0_spmd.clone.clone.sunk | while | flops 1751259136 | bytes 8293444 | solution.py:59
  70.2 1.2 reduce-window.16
  71.4 0.2 slice_reduce_fusion.8
  71.6 0.2 reduce-window.17
  71.8 0.3 fusion.85
  72.2 0.5 constant_dynamic-slice_fusion.2
  72.7 0.1 fusion.86
  72.8 5.2 %fusion.87 = f32[512,4,64]{0,2,1:T(8,128)S(1)} fusion(f32[4,512]{1,0:T(4,128)S(1)} %dynamic-slice_bitcast_fusion.4, f32[512,512]{1,0:T(8,128)S(1)} %fusion.85, f32[4,512]{1,0:T(4,128)S(1)} %bitcast.139, pred[512,512]{1,0:T(8,128)(4,1)S(1)} %fusion.86, f32[1,512,4,64]{1,0,3,2:T(1,128)S(1)} %constant_dynamic-slice_fusion.2), kind=kOutput, calls=%fused_computation.15.clone.1 | convolution fusion | flops 810549248 | bytes 2375680 | tf_op jit(solution)/shard_map/while/body/eval_jaxpr/hts,shp->thp/dot_general | solution.py:46
  78.0 0.2 slice_reduce_fusion.9
  78.3 1.2 fusion.88
  79.5 0.5 convolution_add_fusion.2
  80.1 1.2 reduce-window.16
  81.3 0.2 slice_reduce_fusion.8
  81.5 0.2 reduce-window.17
  81.7 0.3 fusion.85
  82.1 0.5 constant_dynamic-slice_fusion.2
  82.6 0.1 fusion.86
  82.7 5.2 %fusion.87 = f32[512,4,64]{0,2,1:T(8,128)S(1)} fusion(f32[4,512]{1,0:T(4,128)S(1)} %dynamic-slice_bitcast_fusion.4, f32[512,512]{1,0:T(8,128)S(1)} %fusion.85, f32[4,512]{1,0:T(4,128)S(1)} %bitcast.139, pred[512,512]{1,0:T(8,128)(4,1)S(1)} %fusion.86, f32[1,512,4,64]{1,0,3,2:T(1,128)S(1)} %constant_dynamic-slice_fusion.2), kind=kOutput, calls=%fused_computation.15.clone.1 | convolution fusion | flops 810549248 | bytes 2375680 | tf_op jit(solution)/shard_map/while/body/eval_jaxpr/hts,shp->thp/dot_general | solution.py:46
  87.9 0.2 slice_reduce_fusion.9
  88.2 1.2 fusion.88
  89.4 0.5 convolution_add_fusion.2
  89.9 1.6 copy.96
  91.5 0.7 reshape.221
  92.2 3.9 %reduce.16 = bf16[1024,256]{1,0:T(8,128)(2,1)S(1)} reduce(bf16[1024,1,256]{2,1,0:T(2,128)(2,1)S(1)} %reshape.221, bf16[]{:T(256)} %broadcast.101), dimensions={1}, to_apply=%reshape.221.reduce_sub_computation | reduce | bytes 1048578 | tf_op jit(solution)/shard_map/convert_element_type | solution.py:103
  96.1 0.1 reshape.233
  96.2 32.4 %all_to_all.12 = bf16[8,2,16384]{2,1,0:T(2,128)(2,1)S(1)} all-to-all(bf16[8,2,16384]{2,1,0:T(2,128)(2,1)S(1)} %reshape.233), channel_id=1, replica_groups=mesh['ctx'=8,'tp'=4] {'ctx'}, dimensions={0} | all-to-all | bytes 1048576 | tf_op jit(solution)/shard_map/all_to_all | solution.py:104
  128.7 0.5 reshape.234
  129.2 0.1 copy.94
  129.3 0.1 convert_bitcast_fusion
  129.4 0.3 copy.95
  129.8 1.0 copy-done.2
  130.7 0.4 multiply_reduce_fusion
  131.1 173.4 %all-gather.5.cloned.1.call-done = bf16[1,2048,4096]{2,1,0:T(8,128)(2,1)} async-done(((bf16[1,256,4096]{2,1,0:T(8,128)(2,1)}), bf16[1,2048,4096]{2,1,0:T(8,128)(2,1)}) %all-gather.5.cloned.1.call-update) | async-done | bytes 16777232 | tf_op jit(solution)/shard_map/all_gather | solution.py:114
  304.5 9.6 %fusion.47 = f32[128,4096]{1,0:T(8,128)} fusion(bf16[1,2048,4096]{2,1,0:T(8,128)(2,1)} %all-gather.5.cloned.1.call-done, f32[128,1,2048]{0,2,1:T(8,128)S(1)} %get-tuple-element.176, f32[2048]{0:T(1024)S(1)} %bitcast.142, f32[128]{0:T(128)S(1)} %add_rsqrt_fusion), kind=kOutput, calls=%fused_computation.57 | convolution fusion | flops 2148270080 | bytes 19931648 | tf_op jit(solution)/shard_map/tgr,grd->td/dot_general | solution.py:111
  314.1 29.8 %reduce-scatter.2.cloned.1.call-done = f32[128,1024]{1,0:T(8,128)} async-done(((f32[128,4096]{1,0:T(8,128)}), f32[128,1024]{1,0:T(8,128)}) %reduce-scatter.2.cloned.1.call-update) | async-done | bytes 524304 | tf_op jit(solution)/shard_map/reduce_scatter | solution.py:117
  343.9 1.8 convert_element_type.102
  (50 shorter events, 1.0 us)
Async XLA Ops:
  6.5 39.2 %copy-start = (f32[1,32]{1,0:T(1,128)S(1)}, f32[1,32]{1,0:T(1,128)}, u32[]{:S(2)}) copy-start(f32[1,32]{1,0:T(1,128)} %param.13) | copy-start | bytes 388
  6.5 6.5 %copy-start.4 = (f32[1,4,2560]{2,1,0:T(4,128)S(1)}, f32[1,4,2560]{2,1,0:T(4,128)}, u32[]{:S(2)}) copy-start(f32[1,4,2560]{2,1,0:T(4,128)} %param.11) | copy-start | bytes 122884
  6.5 62.3 %all-gather.3.cloned.1.call-start = ((), (), s32[]{:S(2)}) async-start(), calls=%async_computation.4 | async-start | bytes 1179648 | tf_op jit(solution)/shard_map/all_gather | solution.py:89
  7.9 5.3 %slice-start = ((bf16[128,1,4640]{0,2,1:T(8,128)(2,1)}), bf16[128,1,2560]{0,2,1:T(8,128)(2,1)S(1)}, s32[]{:S(2)}) async-start(bf16[128,1,4640]{0,2,1:T(8,128)(2,1)} %param.10), calls=%async_computation.7 | async-start | bytes 1310720 | tf_op jit(solution)/shard_map/slice | solution.py:66
  8.2 6.3 %collective-permute-start = (bf16[3,1,2560]{2,0,1:T(4,128)(2,1)S(1)}, bf16[3,1,2560]{2,0,1:T(4,128)(2,1)S(1)}, u32[]{:S(2)}, u32[]{:S(2)}) collective-permute-start(bf16[3,1,2560]{2,0,1:T(4,128)(2,1)S(1)} %copy.99), channel_id=1, source_target_pairs={{0,4},{4,8},{8,12},{12,16},{16,20},{20,24},{24,28},{1,5},{5,9},{9,... | collective-permute-start | bytes 46088 | tf_op jit(solution)/shard_map/ppermute | solution.py:21
  13.2 0.7 copy-start.5
  15.6 1.5 copy-start.1
  16.3 288.2 %all-gather.5.cloned.1.call-start = ((), (), s32[]{:S(2)}) async-start(), calls=%async_computation.5 | async-start | bytes 18874368 | tf_op jit(solution)/shard_map/all_gather | solution.py:114
  19.6 19.9 %all-to-all-start = ((bf16[8,2,256]{2,1,0:T(2,128)(2,1)}), bf16[8,2,256]{2,1,0:T(2,128)(2,1)S(1)}, u32[]{:S(2)}, u32[]{:S(2)}) async-start(bf16[8,2,256]{2,1,0:T(2,128)(2,1)} %reshape.229), calls=%async_computation | async-start | bytes 16384 | tf_op jit(solution)/shard_map/all_to_all | solution.py:87
  38.5 7.3 %copy-start.6 = (f32[1,32]{1,0:T(1,128)S(1)}, f32[1,32]{1,0:T(1,128)}, u32[]{:S(2)}) copy-start(f32[1,32]{1,0:T(1,128)} %param.14) | copy-start | bytes 388
  39.5 26.5 %all-to-all-start.1 = ((bf16[8,2,16384]{2,1,0:T(2,128)(2,1)}), bf16[8,2,16384]{2,1,0:T(2,128)(2,1)S(1)}, u32[]{:S(2)}, u32[]{:S(2)}) async-start(bf16[8,2,16384]{2,1,0:T(2,128)(2,1)} %reshape.231), calls=%async_computation.1 | async-start | bytes 1048576 | tf_op jit(solution)/shard_map/all_to_all | solution.py:86
  45.5 298.4 %reduce-scatter.2.cloned.1.call-start = ((), (), s32[]{:S(2)}) async-start(), calls=%async_computation.6 | async-start | bytes 2621440 | tf_op jit(solution)/shard_map/reduce_scatter | solution.py:117
  129.4 1.3 copy-start.2
  130.7 173.8 %copy-start.3 = (f32[1,2048]{1,0:T(1,128)S(1)}, f32[1,2048]{1,0:T(1,128)}, u32[]{:S(2)}) copy-start(f32[1,2048]{1,0:T(1,128)} %param.15) | copy-start | bytes 24580
Sparse Core Ops, SparseCore 0:
  16.4 49.3 all-gather.2
  67.9 236.5 all-gather.4
  314.3 29.5 reduce-scatter.1
where the time goes:
time: 353 us; the launch traced here: 352 us
  waiting for transfers between devices  224 us (63%)
  blocking collectives  32.4 us (9%)
  other arithmetic  24.1 us (7%)
  matrix products  24.1 us (7%)
  starting transfers between devices  17.7 us (5%)
  local copies, waits for them, and re-layouts  15.9 us (5%)
  between operations  13.4 us (4%)
    all_gather x1, waiting for transfers between devices, on_device(): lax.all_gather(out_weight, 'ctx', axis=1, tiled=True)  173 us
    all_to_all x1, blocking collectives, on_device(): lax.all_to_all(jnp.stack(pieces_out, axis=1), 'ctx', split_axis=0, concat...  32.4 us
    reduce_scatter x1, waiting for transfers between devices, on_device(): shares = lax.psum_scatter(summed, 'tp', scatter_dimension=1, tiled=True)  29.8 us
    all_to_all x1, waiting for transfers between devices, on_device(): lax.all_to_all(values, 'ctx', split_axis=2, concat_axis=0, tiled=True)  19.9 us
    unnamed x4, other arithmetic  12.2 us
    dot_general x2, matrix products, advance(): jnp.einsum('hts,shp->thp', factors, x_block, precision=highest_precision)  10.4 us
    dot_general x1, matrix products, on_device(): jnp.einsum('tgr,grd->td', normed, lax.all_gather(out_weight, 'ctx', axis=...  9.61 us
  transfers between devices with their start and end apart: 6, of which 4 were waited for; matrix products, arithmetic and copies ran while one was open for 14% of the time, Pallas kernels for 0%

commit v1 on v0

v1 whole, which is shorter than its diff:
```python
import jax
import jax.numpy as jnp
from jax import lax
from jax.sharding import PartitionSpec as P

P_SIZE = 64
N = 256
KCONV = 4
SPAN = 256
GCH = 2048
GCONV = 2560

F32 = jnp.float32
BF16 = jnp.bfloat16
highest_precision = lax.Precision.HIGHEST


def causal_conv(rows, weight, bias):
    count = rows.shape[0]
    padded = jnp.concatenate([jnp.zeros((KCONV - 1, rows.shape[1]), F32), rows.astype(F32)], axis=0)
    total = bias[None]
    for offset in range(KCONV):
        total = total + weight[offset][None] * padded[offset : offset + count]
    return jax.nn.silu(total).astype(BF16)


def ssd(values, steps, decay_rate, b_rows, c_rows, span):
    tokens, heads, width = values.shape
    blocks = tokens // span
    x = values.reshape(blocks, span, heads, width).transpose(0, 2, 1, 3)
    b_blocks = b_rows.reshape(blocks, span, N)
    c_blocks = c_rows.reshape(blocks, span, N)
    step = steps.reshape(blocks, span, heads).transpose(0, 2, 1)
    causal = jnp.arange(span)[:, None] >= jnp.arange(span)[None, :]
    running = jnp.einsum(
        "bhs,ts->bht", step * decay_rate[None, :, None], causal.astype(F32), precision=highest_precision
    )
    cross = jnp.einsum("btn,bsn->bts", c_blocks, b_blocks, preferred_element_type=F32)
    gaps = running[:, :, :, None] - running[:, :, None, :]
    factors = jnp.where(causal, jnp.exp(jnp.where(causal, gaps, 0.0)), 0.0)
    factors = (factors * cross[:, None] * step[:, :, None, :]).astype(BF16)
    within = jnp.einsum("bhts,bhsp->bhtp", factors, x, preferred_element_type=F32)
    tail = jnp.exp(running[:, :, -1:] - running) * step
    weighted = (x.astype(F32) * tail[..., None]).astype(BF16)
    added = jnp.einsum("bhsp,bsn->bhpn", weighted, b_blocks, preferred_element_type=F32)
    kept = jnp.exp(running[:, :, -1])

    def advance(state, piece):
        keep, add = piece
        return state * keep[:, None, None] + add, state

    _, entering = lax.scan(
        advance, jnp.zeros((heads, width, N), F32), (kept, added), unroll=min(blocks, 8)
    )
    carried = jnp.einsum("btn,bhpn->bhtp", c_blocks, entering.astype(BF16), preferred_element_type=F32)
    out = within + carried * jnp.exp(running)[..., None]
    return out.transpose(0, 2, 1, 3).reshape(tokens, heads * width)


def exchange(array, axis, bit):
    peers = lax.axis_size(axis)
    return lax.ppermute(array, axis, [(i, i ^ bit) for i in range(peers)])


def my_bit(axis, bit):
    return (lax.axis_index(axis) // bit) % 2


def bits_of(size):
    return [1 << i for i in range(size.bit_length() - 1)]


def on_device(projected, conv_weight, conv_bias, step_bias, log_rates, norm_gain, out_weight):
    rows = projected.shape[0]
    devices = lax.axis_size("ctx")
    tp = lax.axis_size("tp")
    me = lax.axis_index("ctx")
    width = GCH // devices
    heads = max(1, width // P_SIZE)
    here = projected[:, 0]

    parts = [
        jnp.concatenate(
            [here[:, d * width : (d + 1) * width], here[:, GCH + d * width : GCH + (d + 1) * width]], axis=1
        )
        for d in range(devices)
    ]
    moved = lax.all_to_all(jnp.stack(parts), "ctx", split_axis=0, concat_axis=0, tiled=True)
    tokens = devices * rows
    moved = moved.reshape(tokens, 2 * width)
    shared = lax.all_gather(here[:, 2 * GCH :], "ctx", axis=0, tiled=True)

    first = me * width
    values = causal_conv(
        moved[:, width:],
        lax.dynamic_slice_in_dim(conv_weight[0], first, width, axis=1),
        lax.dynamic_slice_in_dim(conv_bias[0], first, width),
    )
    keys = causal_conv(shared[:, : 2 * N], conv_weight[0, :, GCH:], conv_bias[0, GCH:])
    first_head = first // P_SIZE
    raw = lax.dynamic_slice_in_dim(shared[:, 2 * N :], first_head, heads, axis=1)
    bias = lax.dynamic_slice_in_dim(step_bias[0], first_head, heads)
    rate = -jnp.exp(lax.dynamic_slice_in_dim(log_rates[0], first_head, heads))
    steps = jax.nn.softplus(raw.astype(F32) + bias[None])
    scanned = ssd(
        values.reshape(tokens, heads, width // heads), steps, rate, keys[:, :N], keys[:, N:], SPAN
    ).astype(BF16)

    gated = scanned.astype(F32) * jax.nn.silu(moved[:, :width].astype(F32))
    squares = jnp.sum(gated * gated, axis=1).reshape(devices, rows)
    for bit in bits_of(devices):
        squares = squares + exchange(squares, "ctx", bit)
    scale = lax.rsqrt(squares.reshape(tokens, 1) / GCH + 1e-05)
    gain = lax.dynamic_slice_in_dim(norm_gain[0], first, width)
    normed = (gated * scale * gain[None]).astype(BF16)

    weight = out_weight[0]
    columns = weight.shape[1] // tp
    first_bit = 1
    mine = my_bit("tp", first_bit)

    def product(side, low, size):
        pieces = []
        for high in range(tp // 2):
            begin = (high * 2 + side) * columns + low
            block = lax.dynamic_slice_in_dim(weight, begin, size, axis=1)
            pieces.append(jnp.dot(normed, block, preferred_element_type=F32))
        return jnp.stack(pieces)

    tp_bits = [("tp", bit) for bit in bits_of(tp)[1:]]
    ctx_bits = [("ctx", bit) for bit in bits_of(devices)]
    near, far = ctx_bits[:1], ctx_bits[1:]
    orders = [tp_bits + near + far, near + far + tp_bits, far + tp_bits + near]
    unit = columns // 8
    sizes = [3 * unit, 3 * unit, 2 * unit]
    names = tp_bits[::-1] + ctx_bits[::-1]
    results = []
    low = 0
    for order, size in zip(orders, sizes):
        arrived = exchange(product(1 - mine, low, size).astype(BF16), "tp", first_bit)
        total = product(mine, low, size) + arrived.astype(F32)
        total = total.reshape((2,) * len(names) + (rows, size))
        left = list(names)
        for name in order:
            dim = left.index(name)
            side = my_bit(*name)
            away = lax.dynamic_index_in_dim(total, 1 - side, dim, keepdims=False).astype(BF16)
            stay = lax.dynamic_index_in_dim(total, side, dim, keepdims=False)
            total = stay + exchange(away, *name).astype(F32)
            left.remove(name)
        results.append(total)
        low += size
    return jnp.concatenate(results, axis=1).astype(BF16)


def solution(mesh):
    return jax.shard_map(
        on_device,
        mesh=mesh,
        in_specs=(
            P("ctx", "tp", None),
            P("tp", None, None),
            P("tp", None),
            P("tp", None),
            P("tp", None),
            P("tp", None),
            P("tp", "ctx", None),
        ),
        out_specs=P("ctx", "tp"),
        check_vma=False,
    )
```

time: 353 us -> 190 us (0.54)
  waiting for transfers between devices: 224 us -> 104 us
  blocking collectives: 32.4 us -> 0 us
  matrix products: 24.1 us -> 7.43 us
  local copies, waits for them, and re-layouts: 15.9 us -> 21.4 us
  starting transfers between devices: 17.7 us -> 21.3 us
    all_gather x2 -> x1, waiting for transfers between devices: 173 us -> 12.8 us  [on_device(): shared = lax.all_gather(here[:, 2 * GCH:], 'ctx', axis=0, tiled=True)]
    ppermute x1 -> x18, waiting for transfers between devices: 0.6 us -> 64.5 us  [exchange(): return lax.ppermute(array, axis, [(i, i ^ bit) for i in range(peers)])]
    all_to_all x1 -> x0, blocking collectives: 32.4 us -> none  [on_device(): lax.all_to_all(jnp.stack(pieces_out, axis=1), 'ctx', split_axis=0, concat...]
    reduce_scatter x1 -> x0, waiting for transfers between devices: 29.8 us -> none  [on_device(): shares = lax.psum_scatter(summed, 'tp', scatter_dimension=1, tiled=True)]
    dot_general x9 -> x17, matrix products: 24.1 us -> 7.43 us  [the longest x12 4.74 us: product(): pieces.append(jnp.dot(normed, block, preferred_element_type=F32))]
    ppermute x1 -> x18, starting transfers between devices: 4.87 us -> 14 us  [exchange(): return lax.ppermute(array, axis, [(i, i ^ bit) for i in range(peers)])]
    unnamed x4 -> x7, other arithmetic: 12.2 us -> 4.64 us
    all_to_all x2 -> x1, waiting for transfers between devices: 19.9 us -> 26.7 us  [on_device(): lax.all_to_all(jnp.stack(parts), 'ctx', split_axis=0, concat_axis=0, tile...]
  transfers between devices with their start and end apart: 6 -> 20, of which waited for: 4 -> 12; matrix products, arithmetic and copies ran while one was open for 14% -> 12% of each run, Pallas kernels for 0% -> 0%
where the time goes in v1:
time: 190 us; the launch traced here: 189 us
  waiting for transfers between devices  104 us (55%)
  local copies, waits for them, and re-layouts  21.4 us (11%)
  starting transfers between devices  21.3 us (11%)
  other arithmetic  20.8 us (11%)
  between operations  14 us (7%)
  matrix products  7.43 us (4%)
    ppermute x18, waiting for transfers between devices, exchange(): return lax.ppermute(array, axis, [(i, i ^ bit) for i in range(peers)])  64.5 us
    all_to_all x1, waiting for transfers between devices, on_device(): lax.all_to_all(jnp.stack(parts), 'ctx', split_axis=0, concat_axis=0, tile...  26.7 us
    ppermute x18, starting transfers between devices, exchange(): return lax.ppermute(array, axis, [(i, i ^ bit) for i in range(peers)])  14 us
    all_gather x1, waiting for transfers between devices, on_device(): shared = lax.all_gather(here[:, 2 * GCH:], 'ctx', axis=0, tiled=True)  12.8 us
    all_to_all x1, starting transfers between devices, on_device(): lax.all_to_all(jnp.stack(parts), 'ctx', split_axis=0, concat_axis=0, tile...  7.28 us
    dot_general x12, matrix products, product(): pieces.append(jnp.dot(normed, block, preferred_element_type=F32))  4.74 us
    unnamed x7, other arithmetic  4.64 us
    add x9, other arithmetic, on_device(): total = stay + exchange(away, *name).astype(F32)  4.47 us
  transfers between devices with their start and end apart: 20, of which 12 were waited for; matrix products, arithmetic and copies ran while one was open for 12% of the time, Pallas kernels for 0%

profile of v1, /device:TPU:0, one launch (start us, length us, event | category | flops | bytes accessed | tf_op | source)
XLA Modules:
  0.0 188.9 jit_solution(3927630929335033747)
XLA Ops:
  6.5 1.5 fusion.119
  8.0 0.7 fusion.78
  8.7 0.7 fusion.79
  9.3 0.7 fusion.80
  10.0 0.7 fusion.81
  10.7 0.7 fusion.82
  11.3 0.7 fusion.83
  12.0 0.7 fusion.84
  12.7 0.7 fusion.85
  13.3 7.3 %all-to-all-start = ((bf16[8,128,512]{1,2,0:T(8,128)(2,1)}), bf16[8,128,512]{1,2,0:T(8,128)(2,1)}, u32[]{:S(2)}, u32[]{:S(2)}) async-start(bf16[8,128,512]{1,2,0:T(8,128)(2,1)} %fusion.85), calls=%async_computation | async-start | bytes 2097152 | tf_op jit(solution)/shard_map/all_to_all | solution.py:88
  20.7 1.6 slice.194
  22.4 0.9 constant_dynamic-slice_fusion.2
  23.4 0.9 fusion.121
  24.2 26.7 %all-to-all-done = bf16[8,128,512]{1,2,0:T(8,128)(2,1)} async-done(((bf16[8,128,512]{1,2,0:T(8,128)(2,1)}), bf16[8,128,512]{1,2,0:T(8,128)(2,1)}, u32[]{:S(2)}, u32[]{:S(2)}) %all-to-all-start) | async-done | bytes 1048608 | tf_op jit(solution)/shard_map/all_to_all | solution.py:88
  51.0 1.5 copy.45
  52.5 1.5 multiply_convert_fusion.7
  54.0 2.0 %copy.46 = bf16[1024,256]{0,1:T(8,128)(2,1)} copy(bf16[1024,256]{1,0:T(8,128)(2,1)} %multiply_convert_fusion.7) | data formatting | bytes 1048576 | tf_op jit(solution)/shard_map/convert_element_type | solution.py:24
  56.1 2.3 %reshape_reshape.3 = bf16[4,256,4,64]{1,0,3,2:T(4,128)(2,1)} reshape(bf16[1024,256]{0,1:T(8,128)(2,1)} %copy.46) | data formatting | bytes 1048576 | tf_op jit(solution)/shard_map/reshape;reshape | solution.py:30
  58.3 12.8 %all-gather.2.cloned.1.call-done = bf16[1024,544]{0,1:T(8,128)(2,1)} async-done(((bf16[128,544]{0,1:T(8,128)(2,1)}), bf16[1024,544]{0,1:T(8,128)(2,1)}) %all-gather.2.cloned.1.call-update) | async-done | bytes 1114128 | tf_op jit(solution)/shard_map/all_gather | solution.py:91
  71.1 0.8 slice.195
  72.6 1.5 slice_convert_fusion
  74.0 2.5 %multiply_convert_fusion.2 = bf16[1024,512]{0,1:T(8,128)(2,1)S(1)} fusion(f32[1024,512]{0,1:T(8,128)S(1)} %slice_convert_fusion, f32[512]{0:T(512)S(1)} %bitcast.243, f32[512]{0:T(512)S(1)} %bitcast.241, f32[512]{0:T(512)S(1)} %bitcast.242, f32[512]{0:T(512)S(1)} %bitcast.240, f32[512]{0:T(512)S(1)} %bitcast.239), kind=kLoop, calls=%fused_computation.17 | loop fusion | flops 6815744 | bytes 3155968 | tf_op jit(solution)/shard_map/convert_element_type | solution.py:24
  76.6 1.2 reshape.114
  77.8 1.2 reshape.113
  79.3 0.7 copy-done.6
  80.6 1.4 fusion.14
  82.5 1.8 copy.66
  84.3 2.7 %reshape.124 = f32[1024,256]{1,0:T(8,128)S(1)} reshape(f32[4,256,4,64]{3,2,1,0:T(4,128)} %copy.66) | data formatting | bytes 2097152 | tf_op jit(solution)/shard_map/convert_element_type | solution.py:109
  86.9 1.5 multiply_reduce_fusion
  88.4 1.4 collective-permute-start
  89.8 2.3 %collective-permute-done = f32[8,128]{1,0:T(8,128)S(1)} collective-permute-done((f32[8,128]{1,0:T(8,128)S(1)}, f32[8,128]{1,0:T(8,128)S(1)}, u32[]{:S(2)}, u32[]{:S(2)}) %collective-permute-start) | collective-permute-done | bytes 4128 | tf_op jit(solution)/shard_map/ppermute | solution.py:62
  92.1 0.7 collective-permute-start.1
  92.8 0.7 constant_dynamic-slice_fusion.9
  93.5 2.2 %collective-permute-done.1 = f32[8,128]{1,0:T(8,128)S(1)} collective-permute-done((f32[8,128]{1,0:T(8,128)S(1)}, f32[8,128]{1,0:T(8,128)S(1)}, u32[]{:S(2)}, u32[]{:S(2)}) %collective-permute-start.1) | collective-permute-done | bytes 4128 | tf_op jit(solution)/shard_map/ppermute | solution.py:62
  95.7 1.3 collective-permute-start.2
  97.0 3.2 %collective-permute-done.2 = f32[8,128]{1,0:T(8,128)S(1)} collective-permute-done((f32[8,128]{1,0:T(8,128)S(1)}, f32[8,128]{1,0:T(8,128)S(1)}, u32[]{:S(2)}, u32[]{:S(2)}) %collective-permute-start.2) | collective-permute-done | bytes 4128 | tf_op jit(solution)/shard_map/ppermute | solution.py:62
  100.2 1.4 multiply_convert_fusion.5
  102.4 0.4 fusion.21
  102.9 0.4 fusion.20
  103.5 0.6 collective-permute-start.8
  104.5 0.4 fusion.18
  106.2 0.8 collective-permute-start.14
  107.4 0.4 convolution_bitcast_fusion.1
  107.8 0.4 convolution_bitcast_fusion.2
  108.3 0.4 convolution_bitcast_fusion.3
  108.7 11.8 %collective-permute-done.14 = bf16[2,2,2,128,256]{4,3,2,0,1:T(8,128)(2,1)S(1)} collective-permute-done((bf16[2,2,2,128,256]{4,3,2,0,1:T(8,128)(2,1)S(1)}, bf16[2,2,2,128,256]{4,3,2,0,1:T(8,128)(2,1)S(1)}, u32[]{:S(2)}, u32[]{:S(2)}) %collective-permute-start.14) | collective-permute-done | bytes 524320 | tf_op jit(solution)/shard_map/ppermute | solution.py:62
  120.7 1.4 collective-permute-start.15
  122.5 1.3 collective-permute-start.9
  124.1 11.1 %collective-permute-done.15 = bf16[2,2,128,256]{3,2,1,0:T(8,128)(2,1)S(1)} collective-permute-done((bf16[2,2,128,256]{3,2,1,0:T(8,128)(2,1)S(1)}, bf16[2,2,128,256]{3,2,1,0:T(8,128)(2,1)S(1)}, u32[]{:S(2)}, u32[]{:S(2)}) %collective-permute-start.15) | collective-permute-done | bytes 262176 | tf_op jit(solution)/shard_map/ppermute | solution.py:62
  135.3 1.3 collective-permute-start.16
  136.6 1.0 fusion.30
  137.7 0.7 collective-permute-start.4
  138.4 2.7 %collective-permute-done.16 = bf16[2,128,256]{2,1,0:T(8,128)(2,1)} collective-permute-done((bf16[2,128,256]{2,1,0:T(8,128)(2,1)S(1)}, bf16[2,128,256]{2,1,0:T(8,128)(2,1)}, u32[]{:S(2)}, u32[]{:S(2)}) %collective-permute-start.16) | collective-permute-done | bytes 131104 | tf_op jit(solution)/shard_map/ppermute | solution.py:62
  141.1 0.9 bitcast_add_fusion.8
  142.1 1.3 collective-permute-start.17
  143.3 1.8 bitcast_add_fusion
  145.3 12.3 %collective-permute-done.4 = bf16[2,2,2,128,384]{4,3,0,1,2:T(8,128)(2,1)} collective-permute-done((bf16[2,2,2,128,384]{4,3,0,1,2:T(8,128)(2,1)}, bf16[2,2,2,128,384]{4,3,0,1,2:T(8,128)(2,1)}, u32[]{:S(2)}, u32[]{:S(2)}) %collective-permute-start.4) | collective-permute-done | bytes 786464 | tf_op jit(solution)/shard_map/ppermute | solution.py:62
  157.6 1.3 bitcast_add_fusion.1
  159.0 1.3 collective-permute-start.5
  160.5 8.8 %collective-permute-done.5 = bf16[2,2,128,384]{3,2,0,1:T(8,128)(2,1)S(1)} collective-permute-done((bf16[2,2,128,384]{3,2,0,1:T(8,128)(2,1)S(1)}, bf16[2,2,128,384]{3,2,0,1:T(8,128)(2,1)S(1)}, u32[]{:S(2)}, u32[]{:S(2)}) %collective-permute-start.5) | collective-permute-done | bytes 393248 | tf_op jit(solution)/shard_map/ppermute | solution.py:62
  169.6 1.4 collective-permute-start.12
  171.0 4.1 %collective-permute-done.6 = bf16[2,128,384]{2,1,0:T(8,128)(2,1)S(1)} collective-permute-done((bf16[2,128,384]{2,1,0:T(8,128)(2,1)S(1)}, bf16[2,128,384]{2,1,0:T(8,128)(2,1)S(1)}, u32[]{:S(2)}, u32[]{:S(2)}) %collective-permute-start.6) | collective-permute-done | bytes 196640 | tf_op jit(solution)/shard_map/ppermute | solution.py:62
  175.4 6.0 %collective-permute-done.7 = bf16[128,384]{1,0:T(8,128)(2,1)S(1)} collective-permute-done((bf16[128,384]{1,0:T(8,128)(2,1)S(1)}, bf16[128,384]{1,0:T(8,128)(2,1)S(1)}, u32[]{:S(2)}, u32[]{:S(2)}) %collective-permute-start.7) | collective-permute-done | bytes 98336 | tf_op jit(solution)/shard_map/ppermute | solution.py:62
  181.3 0.7 pad_maximum_fusion.3
  (92 shorter events, 7.1 us)
Async XLA Ops:
  6.5 95.1 %copy-start = (bf16[1,256,4096]{2,1,0:T(8,128)(2,1)S(1)}, bf16[1,256,4096]{2,1,0:T(8,128)(2,1)}, u32[]{:S(2)}) copy-start(bf16[1,256,4096]{2,1,0:T(8,128)(2,1)} %param.13) | copy-start | bytes 6291460
  9.3 13.0 %copy-start.8 = (f32[1,2560]{1,0:T(1,128)S(1)}, f32[1,2560]{1,0:T(1,128)}, u32[]{:S(2)}) copy-start(f32[1,2560]{1,0:T(1,128)} %param.9) | copy-start | bytes 30724
  9.3 13.0 %copy-start.9 = (f32[1,32]{1,0:T(1,128)S(1)}, f32[1,32]{1,0:T(1,128)}, u32[]{:S(2)}) copy-start(f32[1,32]{1,0:T(1,128)} %param.10) | copy-start | bytes 388
  9.3 13.0 %copy-start.10 = (f32[1,32]{1,0:T(1,128)S(1)}, f32[1,32]{1,0:T(1,128)}, u32[]{:S(2)}) copy-start(f32[1,32]{1,0:T(1,128)} %param.11) | copy-start | bytes 388
  13.3 37.6 %all-to-all-start = ((bf16[8,128,512]{1,2,0:T(8,128)(2,1)}), bf16[8,128,512]{1,2,0:T(8,128)(2,1)}, u32[]{:S(2)}, u32[]{:S(2)}) async-start(bf16[8,128,512]{1,2,0:T(8,128)(2,1)} %fusion.85), calls=%async_computation | async-start | bytes 2097152 | tf_op jit(solution)/shard_map/all_to_all | solution.py:88
  20.6 50.5 %all-gather.2.cloned.1.call-start = ((), (), s32[]{:S(2)}) async-start(), calls=%async_computation.1 | async-start | bytes 1253376 | tf_op jit(solution)/shard_map/all_gather | solution.py:91
  52.5 3.6 %copy-start.4 = (bf16[8,128,512]{2,1,0:T(8,128)(2,1)}, bf16[8,128,512]{2,1,0:T(8,128)(2,1)S(1)}, u32[]{:S(2)}) copy-start(bf16[8,128,512]{2,1,0:T(8,128)(2,1)S(1)} %copy.45) | copy-start | bytes 3145732
  56.1 18.0 %slice-start = ((f32[1,2560]{1,0:T(1,128)}), f32[1,512]{1,0:T(1,128)S(1)}, s32[]{:S(2)}) async-start(f32[1,2560]{1,0:T(1,128)} %param.9), calls=%async_computation.2 | async-start | bytes 4096 | tf_op jit(solution)/shard_map/slice | solution.py:99
  78.9 1.0 copy-start.6
  78.9 1.3 copy-start.7
  80.5 1.6 copy-start.5
  88.4 3.7 %collective-permute-start = (f32[8,128]{1,0:T(8,128)S(1)}, f32[8,128]{1,0:T(8,128)S(1)}, u32[]{:S(2)}, u32[]{:S(2)}) collective-permute-start(f32[8,128]{1,0:T(8,128)S(1)} %bitcast.238), channel_id=1, source_target_pairs={{0,4},{4,0},{8,12},{12,8},{16,20},{20,16},{24,28},{28,24},{1,5},{5... | collective-permute-start | bytes 12296 | tf_op jit(solution)/shard_map/ppermute | solution.py:62
  92.1 3.6 %collective-permute-start.1 = (f32[8,128]{1,0:T(8,128)S(1)}, f32[8,128]{1,0:T(8,128)S(1)}, u32[]{:S(2)}, u32[]{:S(2)}) collective-permute-start(f32[8,128]{1,0:T(8,128)S(1)} %bitcast_add_fusion.12), channel_id=1, source_target_pairs={{0,8},{4,12},{8,0},{12,4},{16,24},{20,28},{24,16},{28,20},{1,9},{5... | collective-permute-start | bytes 12296 | tf_op jit(solution)/shard_map/ppermute | solution.py:62
  95.7 4.5 %collective-permute-start.2 = (f32[8,128]{1,0:T(8,128)S(1)}, f32[8,128]{1,0:T(8,128)S(1)}, u32[]{:S(2)}, u32[]{:S(2)}) collective-permute-start(f32[8,128]{1,0:T(8,128)S(1)} %fusion.134), channel_id=1, source_target_pairs={{0,16},{4,20},{8,24},{12,28},{16,0},{20,4},{24,8},{28,12},{1,17},{... | collective-permute-start | bytes 12296 | tf_op jit(solution)/shard_map/ppermute | solution.py:62
  102.3 3.5 %collective-permute-start.13 = (bf16[2,1024,256]{2,1,0:T(8,128)(2,1)S(1)}, bf16[2,1024,256]{2,1,0:T(8,128)(2,1)S(1)}, u32[]{:S(2)}, u32[]{:S(2)}) collective-permute-start(bf16[2,1024,256]{2,1,0:T(8,128)(2,1)S(1)} %pad_maximum_fusion.2), channel_id=1, source_target_pairs={{0,1},{1,0},{2,3},{3,2},{4,5},{5,4},{6,7},{7,6},{8,9},{9,8},{10,11... | collective-permute-start | bytes 3145736 | tf_op jit(solution)/shard_map/ppermute | solution.py:62
  103.5 18.6 %collective-permute-start.8 = (bf16[2,1024,384]{2,1,0:T(8,128)(2,1)S(1)}, bf16[2,1024,384]{2,1,0:T(8,128)(2,1)S(1)}, u32[]{:S(2)}, u32[]{:S(2)}) collective-permute-start(bf16[2,1024,384]{2,1,0:T(8,128)(2,1)S(1)} %pad_maximum_fusion.1), channel_id=1, source_target_pairs={{0,1},{1,0},{2,3},{3,2},{4,5},{5,4},{6,7},{7,6},{8,9},{9,8},{10,11... | collective-permute-start | bytes 4718600 | tf_op jit(solution)/shard_map/ppermute | solution.py:62
  105.4 18.3 %collective-permute-start.3 = (bf16[2,1024,384]{2,1,0:T(8,128)(2,1)S(1)}, bf16[2,1024,384]{2,1,0:T(8,128)(2,1)S(1)}, u32[]{:S(2)}, u32[]{:S(2)}) collective-permute-start(bf16[2,1024,384]{2,1,0:T(8,128)(2,1)S(1)} %pad_maximum_fusion), channel_id=1, source_target_pairs={{0,1},{1,0},{2,3},{3,2},{4,5},{5,4},{6,7},{7,6},{8,9},{9,8},{10,11... | collective-permute-start | bytes 4718600 | tf_op jit(solution)/shard_map/ppermute | solution.py:62
  106.2 14.4 %collective-permute-start.14 = (bf16[2,2,2,128,256]{4,3,2,0,1:T(8,128)(2,1)S(1)}, bf16[2,2,2,128,256]{4,3,2,0,1:T(8,128)(2,1)S(1)}, u32[]{:S(2)}, u32[]{:S(2)}) collective-permute-start(bf16[2,2,2,128,256]{4,3,2,0,1:T(8,128)(2,1)S(1)} %fusion.32), channel_id=1, source_target_pairs={{0,8},{4,12},{8,0},{12,4},{16,24},{20,28},{24,16},{28,20},{1,9},{5... | collective-permute-start | bytes 1572872 | tf_op jit(solution)/shard_map/ppermute | solution.py:62
  120.7 14.5 %collective-permute-start.15 = (bf16[2,2,128,256]{3,2,1,0:T(8,128)(2,1)S(1)}, bf16[2,2,128,256]{3,2,1,0:T(8,128)(2,1)S(1)}, u32[]{:S(2)}, u32[]{:S(2)}) collective-permute-start(bf16[2,2,128,256]{3,2,1,0:T(8,128)(2,1)S(1)} %fusion.51), channel_id=1, source_target_pairs={{0,16},{4,20},{8,24},{12,28},{16,0},{20,4},{24,8},{28,12},{1,17},{... | collective-permute-start | bytes 786440 | tf_op jit(solution)/shard_map/ppermute | solution.py:62
  122.4 1.7 copy-start.1
  122.5 20.8 %collective-permute-start.9 = (bf16[2,2,2,128,384]{4,3,0,1,2:T(8,128)(2,1)S(1)}, bf16[2,2,2,128,384]{4,3,0,1,2:T(8,128)(2,1)}, u32[]{:S(2)}, u32[]{:S(2)}) collective-permute-start(bf16[2,2,2,128,384]{4,3,0,1,2:T(8,128)(2,1)S(1)} %fusion.31), channel_id=1, source_target_pairs={{0,4},{4,0},{8,12},{12,8},{16,20},{20,16},{24,28},{28,24},{1,5},{5... | collective-permute-start | bytes 2359304 | tf_op jit(solution)/shard_map/ppermute | solution.py:62
  124.1 12.6 %copy-start.2 = (f32[2,1024,384]{2,1,0:T(8,128)}, f32[2,1024,384]{2,1,0:T(8,128)S(1)}, u32[]{:S(2)}) copy-start(f32[2,1024,384]{2,1,0:T(8,128)S(1)} %maximum_add_fusion) | copy-start | bytes 9437188
  135.3 5.8 %collective-permute-start.16 = (bf16[2,128,256]{2,1,0:T(8,128)(2,1)S(1)}, bf16[2,128,256]{2,1,0:T(8,128)(2,1)}, u32[]{:S(2)}, u32[]{:S(2)}) collective-permute-start(bf16[2,128,256]{2,1,0:T(8,128)(2,1)S(1)} %fusion.77), channel_id=1, source_target_pairs={{0,2},{1,3},{2,0},{3,1},{4,6},{5,7},{6,4},{7,5},{8,10},{9,11},{10,... | collective-permute-start | bytes 393224 | tf_op jit(solution)/shard_map/ppermute | solution.py:62
  137.7 19.9 %collective-permute-start.4 = (bf16[2,2,2,128,384]{4,3,0,1,2:T(8,128)(2,1)}, bf16[2,2,2,128,384]{4,3,0,1,2:T(8,128)(2,1)}, u32[]{:S(2)}, u32[]{:S(2)}) collective-permute-start(bf16[2,2,2,128,384]{4,3,0,1,2:T(8,128)(2,1)} %fusion.30), channel_id=1, source_target_pairs={{0,2},{1,3},{2,0},{3,1},{4,6},{5,7},{6,4},{7,5},{8,10},{9,11},{10,... | collective-permute-start | bytes 2359304 | tf_op jit(solution)/shard_map/ppermute | solution.py:62
  142.0 15.5 %copy-start.3 = (f32[2,1024,384]{2,1,0:T(8,128)S(1)}, f32[2,1024,384]{2,1,0:T(8,128)}, u32[]{:S(2)}) copy-start(f32[2,1024,384]{2,1,0:T(8,128)} %copy-done.2) | copy-start | bytes 9437188
  142.1 18.3 %collective-permute-start.17 = (bf16[128,256]{1,0:T(8,128)(2,1)S(1)}, bf16[128,256]{1,0:T(8,128)(2,1)S(1)}, u32[]{:S(2)}, u32[]{:S(2)}) collective-permute-start(bf16[128,256]{1,0:T(8,128)(2,1)S(1)} %fusion.97), channel_id=1, source_target_pairs={{0,4},{4,0},{8,12},{12,8},{16,20},{20,16},{24,28},{28,24},{1,5},{5... | collective-permute-start | bytes 196616 | tf_op jit(solution)/shard_map/ppermute | solution.py:62
  145.2 15.1 %collective-permute-start.10 = (bf16[2,2,128,384]{3,2,0,1:T(8,128)(2,1)S(1)}, bf16[2,2,128,384]{3,2,0,1:T(8,128)(2,1)S(1)}, u32[]{:S(2)}, u32[]{:S(2)}) collective-permute-start(bf16[2,2,128,384]{3,2,0,1:T(8,128)(2,1)S(1)} %fusion.50), channel_id=1, source_target_pairs={{0,8},{4,12},{8,0},{12,4},{16,24},{20,28},{24,16},{28,20},{1,9},{5... | collective-permute-start | bytes 1179656 | tf_op jit(solution)/shard_map/ppermute | solution.py:62
  159.0 10.3 %collective-permute-start.5 = (bf16[2,2,128,384]{3,2,0,1:T(8,128)(2,1)S(1)}, bf16[2,2,128,384]{3,2,0,1:T(8,128)(2,1)S(1)}, u32[]{:S(2)}, u32[]{:S(2)}) collective-permute-start(bf16[2,2,128,384]{3,2,0,1:T(8,128)(2,1)S(1)} %fusion.49), channel_id=1, source_target_pairs={{0,4},{4,0},{8,12},{12,8},{16,20},{20,16},{24,28},{28,24},{1,5},{5... | collective-permute-start | bytes 1179656 | tf_op jit(solution)/shard_map/ppermute | solution.py:62
  160.5 9.1 %collective-permute-start.11 = (bf16[2,128,384]{2,1,0:T(8,128)(2,1)S(1)}, bf16[2,128,384]{2,1,0:T(8,128)(2,1)S(1)}, u32[]{:S(2)}, u32[]{:S(2)}) collective-permute-start(bf16[2,128,384]{2,1,0:T(8,128)(2,1)S(1)} %fusion.58), channel_id=1, source_target_pairs={{0,16},{4,20},{8,24},{12,28},{16,0},{20,4},{24,8},{28,12},{1,17},{... | collective-permute-start | bytes 589832 | tf_op jit(solution)/shard_map/ppermute | solution.py:62
  169.4 5.7 %collective-permute-start.6 = (bf16[2,128,384]{2,1,0:T(8,128)(2,1)S(1)}, bf16[2,128,384]{2,1,0:T(8,128)(2,1)S(1)}, u32[]{:S(2)}, u32[]{:S(2)}) collective-permute-start(bf16[2,128,384]{2,1,0:T(8,128)(2,1)S(1)} %fusion.57), channel_id=1, source_target_pairs={{0,8},{4,12},{8,0},{12,4},{16,24},{20,28},{24,16},{28,20},{1,9},{5... | collective-permute-start | bytes 589832 | tf_op jit(solution)/shard_map/ppermute | solution.py:62
  169.6 5.7 %collective-permute-start.12 = (bf16[128,384]{1,0:T(8,128)(2,1)S(1)}, bf16[128,384]{1,0:T(8,128)(2,1)S(1)}, u32[]{:S(2)}, u32[]{:S(2)}) collective-permute-start(bf16[128,384]{1,0:T(8,128)(2,1)S(1)} %fusion.96), channel_id=1, source_target_pairs={{0,2},{1,3},{2,0},{3,1},{4,6},{5,7},{6,4},{7,5},{8,10},{9,11},{10,... | collective-permute-start | bytes 294920 | tf_op jit(solution)/shard_map/ppermute | solution.py:62
  175.2 6.1 %collective-permute-start.7 = (bf16[128,384]{1,0:T(8,128)(2,1)S(1)}, bf16[128,384]{1,0:T(8,128)(2,1)S(1)}, u32[]{:S(2)}, u32[]{:S(2)}) collective-permute-start(bf16[128,384]{1,0:T(8,128)(2,1)S(1)} %fusion.95), channel_id=1, source_target_pairs={{0,16},{4,20},{8,24},{12,28},{16,0},{20,4},{24,8},{28,12},{1,17},{... | collective-permute-start | bytes 294920 | tf_op jit(solution)/shard_map/ppermute | solution.py:62
Sparse Core Ops, SparseCore 0:
  23.5 47.5 all-gather.1

commit v2 on v1

--- a/solution.py
+++ b/solution.py
@@ -70,6 +70,33 @@
     return [1 << i for i in range(size.bit_length() - 1)]
 
 
+def gather_tokens(rows, order):
+    whole = rows
+    held = []
+    for bit in order:
+        other = exchange(whole, "ctx", bit)
+        place = sum(1 for done in held if done > bit)
+        own_first = jnp.stack([whole, other], axis=place)
+        own_last = jnp.stack([other, whole], axis=place)
+        whole = jnp.where(my_bit("ctx", bit) == 0, own_first, own_last)
+        held.append(bit)
+    return whole
+
+
+def to_channels(columns, devices, me, width):
+    rows = columns.shape[0]
+    if devices > 8:
+        pieces = columns.reshape(rows, devices, width).transpose(1, 0, 2)
+        return lax.all_to_all(pieces, "ctx", split_axis=0, concat_axis=0, tiled=True).reshape(-1, width)
+    whole = jnp.zeros((devices * rows, width), columns.dtype)
+    for m in range(devices):
+        piece = lax.dynamic_slice_in_dim(columns, (me ^ m) * width, width, axis=1)
+        if m > 0:
+            piece = exchange(piece, "ctx", m)
+        whole = lax.dynamic_update_slice_in_dim(whole, piece, (me ^ m) * rows, axis=0)
+    return whole
+
+
 def on_device(projected, conv_weight, conv_bias, step_bias, log_rates, norm_gain, out_weight):
     rows = projected.shape[0]
     devices = lax.axis_size("ctx")
@@ -79,37 +106,40 @@
     heads = max(1, width // P_SIZE)
     here = projected[:, 0]
 
-    parts = [
-        jnp.concatenate(
-            [here[:, d * width : (d + 1) * width], here[:, GCH + d * width : GCH + (d + 1) * width]], axis=1
-        )
-        for d in range(devices)
-    ]
-    moved = lax.all_to_all(jnp.stack(parts), "ctx", split_axis=0, concat_axis=0, tiled=True)
     tokens = devices * rows
-    moved = moved.reshape(tokens, 2 * width)
-    shared = lax.all_gather(here[:, 2 * GCH :], "ctx", axis=0, tiled=True)
+    tail_columns = here[:, 2 * GCH :]
+    orders = [bits_of(devices)[::-1], bits_of(devices)[::-1]]
+    if devices > 2:
+        orders[0] = orders[0][:1] + orders[0][1:][::-1]
+    b_raw = gather_tokens(tail_columns[:, :N], orders[0]).reshape(tokens, N)
+    rest_raw = gather_tokens(tail_columns[:, N:], orders[1]).reshape(tokens, -1)
+    x_raw = to_channels(here[:, GCH : 2 * GCH], devices, me, width)
+    z_raw = to_channels(here[:, :GCH], devices, me, width)
 
     first = me * width
     values = causal_conv(
-        moved[:, width:],
+        x_raw,
         lax.dynamic_slice_in_dim(conv_weight[0], first, width, axis=1),
         lax.dynamic_slice_in_dim(conv_bias[0], first, width),
     )
-    keys = causal_conv(shared[:, : 2 * N], conv_weight[0, :, GCH:], conv_bias[0, GCH:])
+    b_keys = causal_conv(b_raw, conv_weight[0, :, GCH : GCH + N], conv_bias[0, GCH : GCH + N])
+    c_keys = causal_conv(rest_raw[:, :N], conv_weight[0, :, GCH + N :], conv_bias[0, GCH + N :])
     first_head = first // P_SIZE
-    raw = lax.dynamic_slice_in_dim(shared[:, 2 * N :], first_head, heads, axis=1)
+    raw = lax.dynamic_slice_in_dim(rest_raw[:, N:], first_head, heads, axis=1)
     bias = lax.dynamic_slice_in_dim(step_bias[0], first_head, heads)
     rate = -jnp.exp(lax.dynamic_slice_in_dim(log_rates[0], first_head, heads))
     steps = jax.nn.softplus(raw.astype(F32) + bias[None])
     scanned = ssd(
-        values.reshape(tokens, heads, width // heads), steps, rate, keys[:, :N], keys[:, N:], SPAN
+        values.reshape(tokens, heads, width // heads), steps, rate, b_keys, c_keys, SPAN
     ).astype(BF16)
 
-    gated = scanned.astype(F32) * jax.nn.silu(moved[:, :width].astype(F32))
+    gated = scanned.astype(F32) * jax.nn.silu(z_raw.astype(F32))
     squares = jnp.sum(gated * gated, axis=1).reshape(devices, rows)
-    for bit in bits_of(devices):
-        squares = squares + exchange(squares, "ctx", bit)
+    radix = 1
+    while radix < devices:
+        reach = min(8, devices // radix)
+        squares = squares + sum(exchange(squares, "ctx", radix * m) for m in range(1, reach))
+        radix *= reach
     scale = lax.rsqrt(squares.reshape(tokens, 1) / GCH + 1e-05)
     gain = lax.dynamic_slice_in_dim(norm_gain[0], first, width)
     normed = (gated * scale * gain[None]).astype(BF16)
@@ -134,22 +164,29 @@
     unit = columns // 8
     sizes = [3 * unit, 3 * unit, 2 * unit]
     names = tp_bits[::-1] + ctx_bits[::-1]
-    results = []
-    low = 0
-    for order, size in zip(orders, sizes):
-        arrived = exchange(product(1 - mine, low, size).astype(BF16), "tp", first_bit)
-        total = product(mine, low, size) + arrived.astype(F32)
-        total = total.reshape((2,) * len(names) + (rows, size))
-        left = list(names)
-        for name in order:
-            dim = left.index(name)
+    lows = [0, sizes[0], sizes[0] + sizes[1]]
+    leaving = [product(1 - mine, low, size).astype(BF16) for low, size in zip(lows, sizes)]
+    arrived = lax.optimization_barrier([exchange(part, "tp", first_bit) for part in leaving])
+    totals = [
+        (product(mine, low, size) + part.astype(F32)).reshape((2,) * len(names) + (rows, size))
+        for low, size, part in zip(lows, sizes, arrived)
+    ]
+    left = [list(names) for _ in orders]
+    for stage in range(len(names)):
+        aways, stays = [], []
+        for index, order in enumerate(orders):
+            name = order[stage]
+            dim = left[index].index(name)
             side = my_bit(*name)
-            away = lax.dynamic_index_in_dim(total, 1 - side, dim, keepdims=False).astype(BF16)
-            stay = lax.dynamic_index_in_dim(total, side, dim, keepdims=False)
-            total = stay + exchange(away, *name).astype(F32)
-            left.remove(name)
-        results.append(total)
-        low += size
+            away = lax.dynamic_index_in_dim(totals[index], 1 - side, dim, keepdims=False)
+            aways.append(away.astype(BF16))
+            stays.append(lax.dynamic_index_in_dim(totals[index], side, dim, keepdims=False))
+            left[index].remove(name)
+        aways = lax.optimization_barrier(aways)
+        arrived = [exchange(away, *order[stage]) for away, order in zip(aways, orders)]
+        arrived = lax.optimization_barrier(arrived)
+        totals = [stay + part.astype(F32) for stay, part in zip(stays, arrived)]
+    results = totals
     return jnp.concatenate(results, axis=1).astype(BF16)
 
 

time: 190 us -> 212 us (1.12)
  starting transfers between devices: 21.3 us -> 52.8 us
  waiting for transfers between devices: 104 us -> 76.9 us
  other arithmetic: 20.8 us -> 36.6 us
  local copies, waits for them, and re-layouts: 21.4 us -> 35.1 us
  between operations: 14 us -> 0.92 us
    ppermute x18 -> x42, starting transfers between devices: 14 us -> 52.8 us  [exchange(): return lax.ppermute(array, axis, [(i, i ^ bit) for i in range(peers)])]
    all_to_all x1 -> x0, waiting for transfers between devices: 26.7 us -> none  [on_device(): lax.all_to_all(jnp.stack(parts), 'ctx', split_axis=0, concat_axis=0, tile...]
    all_gather x1 -> x0, waiting for transfers between devices: 12.8 us -> none  [on_device(): shared = lax.all_gather(here[:, 2 * GCH:], 'ctx', axis=0, tiled=True)]
    ppermute x18 -> x42, waiting for transfers between devices: 64.5 us -> 76.9 us  [exchange(): return lax.ppermute(array, axis, [(i, i ^ bit) for i in range(peers)])]
    add x14 -> x12, other arithmetic: 5.25 us -> 14.5 us  [the longest x9 7.94 us: on_device(): totals = [stay + part.astype(F32) for stay, part in zip(stays, arrived)]]
    all_to_all x1 -> x0, starting transfers between devices: 7.28 us -> none  [on_device(): lax.all_to_all(jnp.stack(parts), 'ctx', split_axis=0, concat_axis=0, tile...]
    unnamed x7 -> x0, other arithmetic: 4.64 us -> none
    select_n x0 -> x2, local copies, waits for them, and re-layouts: none -> 4.24 us  [gather_tokens(): whole = jnp.where(my_bit('ctx', bit) == 0, own_first, own_last)]
  transfers between devices with their start and end apart: 20 -> 42, of which waited for: 12 -> 21; matrix products, arithmetic and copies ran while one was open for 12% -> 17% of each run, Pallas kernels for 0% -> 0%
where the time goes in v2:
time: 212 us; the launch traced here: 211 us
  waiting for transfers between devices  76.9 us (36%)
  starting transfers between devices  52.8 us (25%)
  other arithmetic  36.6 us (17%)
  local copies, waits for them, and re-layouts  35.1 us (17%)
  matrix products  8.92 us (4%)
    ppermute x42, waiting for transfers between devices, exchange(): return lax.ppermute(array, axis, [(i, i ^ bit) for i in range(peers)])  76.9 us
    ppermute x42, starting transfers between devices, exchange(): return lax.ppermute(array, axis, [(i, i ^ bit) for i in range(peers)])  52.8 us
    add x9, other arithmetic, on_device(): totals = [stay + part.astype(F32) for stay, part in zip(stays, arrived)]  7.94 us
    convert_element_type x3, other arithmetic, causal_conv(): return jax.nn.silu(total).astype(BF16)  6.98 us
    add x3, other arithmetic, on_device(): product(mine, low, size) + part.astype(F32)  6.51 us
    dot_general x12, matrix products, product(): pieces.append(jnp.dot(normed, block, preferred_element_type=F32))  5.15 us
    convert_element_type x2, local copies, waits for them, and re-layouts, causal_conv(): rows.astype(F32)  5.09 us
    select_n x2, local copies, waits for them, and re-layouts, gather_tokens(): whole = jnp.where(my_bit('ctx', bit) == 0, own_first, own_last)  4.24 us
  transfers between devices with their start and end apart: 42, of which 21 were waited for; matrix products, arithmetic and copies ran while one was open for 17% of the time, Pallas kernels for 0%

profile of v2, /device:TPU:0, one launch (start us, length us, event | category | flops | bytes accessed | tf_op | source)
XLA Modules:
  0.0 211.3 jit_solution(4859317685177439608)
XLA Ops:
  0.0 1.7 slice_bitcast_fusion.5
  1.7 4.0 %collective-permute-start = (bf16[128,288]{0,1:T(8,128)(2,1)}, bf16[128,288]{0,1:T(8,128)(2,1)S(1)}, u32[]{:S(2)}, u32[]{:S(2)}) collective-permute-start(bf16[128,288]{0,1:T(8,128)(2,1)} %get-tuple-element.66), channel_id=1, source_target_pairs={{0,16},{4,20},{8,24},{12,28},{16,0},{20,4},{24,8},{28,12},{1,17},{... | collective-permute-start | bytes 221192 | tf_op jit(solution)/shard_map/ppermute | solution.py:62
  5.8 1.5 slice_bitcast_fusion.3
  7.3 2.1 fusion.121
  9.4 1.9 constant_dynamic-slice_fusion.9
  11.3 1.9 collective-permute-start.13
  13.2 1.6 collective-permute-start.14
  15.5 1.3 constant_dynamic-slice_fusion.25
  17.4 1.5 constant_dynamic-slice_fusion.1
  18.9 1.3 fusion.114
  20.3 2.9 %collective-permute-start.16 = (bf16[128,256]{0,1:T(8,128)(2,1)}, bf16[128,256]{0,1:T(8,128)(2,1)S(1)}, u32[]{:S(2)}, u32[]{:S(2)}) collective-permute-start(bf16[128,256]{0,1:T(8,128)(2,1)} %get-tuple-element.73), channel_id=1, source_target_pairs={{0,16},{4,20},{8,24},{12,28},{16,0},{20,4},{24,8},{28,12},{1,17},{... | collective-permute-start | bytes 196616 | tf_op jit(solution)/shard_map/ppermute | solution.py:62
  23.9 1.6 collective-permute-start.6
  26.3 1.8 collective-permute-done.6
  28.1 1.3 collective-permute-start.17
  29.5 1.6 collective-permute-start.7
  32.0 1.8 collective-permute-done.7
  33.8 4.7 %collective-permute-start.18 = (bf16[128,256]{0,1:T(8,128)(2,1)S(1)}, bf16[128,256]{0,1:T(8,128)(2,1)S(1)}, u32[]{:S(2)}, u32[]{:S(2)}) collective-permute-start(bf16[128,256]{0,1:T(8,128)(2,1)S(1)} %copy-done.15), channel_id=1, source_target_pairs={{0,24},{4,28},{8,16},{12,20},{16,8},{20,12},{24,0},{28,4},{1,25},{... | collective-permute-start | bytes 196616 | tf_op jit(solution)/shard_map/ppermute | solution.py:62
  38.7 5.2 %collective-permute-done.8 = bf16[128,256]{0,1:T(8,128)(2,1)S(1)} collective-permute-done((bf16[128,256]{0,1:T(8,128)(2,1)S(1)}, bf16[128,256]{0,1:T(8,128)(2,1)S(1)}, u32[]{:S(2)}, u32[]{:S(2)}) %collective-permute-start.8) | collective-permute-done | bytes 65568 | tf_op jit(solution)/shard_map/ppermute | solution.py:62
  44.5 1.9 collective-permute-start.9
  46.5 6.5 %collective-permute-done.9 = bf16[128,256]{0,1:T(8,128)(2,1)S(1)} collective-permute-done((bf16[128,256]{0,1:T(8,128)(2,1)S(1)}, bf16[128,256]{0,1:T(8,128)(2,1)S(1)}, u32[]{:S(2)}, u32[]{:S(2)}) %collective-permute-start.9) | collective-permute-done | bytes 65568 | tf_op jit(solution)/shard_map/ppermute | solution.py:62
  53.1 1.6 collective-permute-start.11
  54.7 5.2 %collective-permute-done.10 = bf16[128,256]{0,1:T(8,128)(2,1)S(1)} collective-permute-done((bf16[128,256]{0,1:T(8,128)(2,1)S(1)}, bf16[128,256]{0,1:T(8,128)(2,1)S(1)}, u32[]{:S(2)}, u32[]{:S(2)}) %collective-permute-start.10) | collective-permute-done | bytes 65568 | tf_op jit(solution)/shard_map/ppermute | solution.py:62
  59.9 2.2 %collective-permute-start.12 = (bf16[128,256]{0,1:T(8,128)(2,1)S(1)}, bf16[128,256]{0,1:T(8,128)(2,1)S(1)}, u32[]{:S(2)}, u32[]{:S(2)}) collective-permute-start(bf16[128,256]{0,1:T(8,128)(2,1)S(1)} %get-tuple-element.78), channel_id=1, source_target_pairs={{0,28},{4,24},{8,20},{12,16},{16,12},{20,8},{24,4},{28,0},{1,29},{... | collective-permute-start | bytes 196616 | tf_op jit(solution)/shard_map/ppermute | solution.py:62
  62.4 5.2 %collective-permute-done.12 = bf16[128,256]{0,1:T(8,128)(2,1)S(1)} collective-permute-done((bf16[128,256]{0,1:T(8,128)(2,1)S(1)}, bf16[128,256]{0,1:T(8,128)(2,1)S(1)}, u32[]{:S(2)}, u32[]{:S(2)}) %collective-permute-start.12) | collective-permute-done | bytes 65568 | tf_op jit(solution)/shard_map/ppermute | solution.py:62
  67.7 1.2 multiply_convert_fusion.6
  68.9 1.2 reshape_reshape.3
  71.3 2.1 collective-permute-start.5
  73.4 2.9 %collective-permute-done.1 = bf16[2,128,288]{1,2,0:T(8,128)(2,1)S(1)} collective-permute-done((bf16[2,128,288]{1,2,0:T(8,128)(2,1)S(1)}, bf16[2,128,288]{1,2,0:T(8,128)(2,1)S(1)}, u32[]{:S(2)}, u32[]{:S(2)}) %collective-permute-start.1) | collective-permute-done | bytes 147488 | tf_op jit(solution)/shard_map/ppermute | solution.py:62
  80.3 2.5 %copy.17 = f32[2,2,2,128,256]{4,3,2,1,0:T(8,128)} copy(f32[2,2,2,128,256]{3,4,0,2,1:T(8,128)} %fusion.48) | data formatting | bytes 2097152 | tf_op jit(solution)/shard_map/convert_element_type | solution.py:20
  82.8 2.6 %copy.18 = f32[1024,256]{0,1:T(8,128)} copy(f32[1024,256]{1,0:T(8,128)} %bitcast.230) | data formatting | bytes 2097152 | tf_op jit(solution)/shard_map/convert_element_type | solution.py:20
  85.4 3.8 %multiply_convert_fusion.7 = bf16[1024,256]{0,1:T(8,128)(2,1)S(1)} fusion(f32[1024,256]{0,1:T(8,128)} %copy.18, f32[256]{0:T(256)S(1)} %bitcast.269, f32[256]{0:T(256)S(1)} %bitcast.266, f32[256]{0:T(256)S(1)} %bitcast.267, f32[256]{0:T(256)S(1)} %bitcast.268, f32[256]{0:T(256)S(1)} %bitcast.260), kind=kLoop, calls=%fused_computation.83 | loop fusion | flops 3407872 | bytes 1577984 | tf_op jit(solution)/shard_map/convert_element_type | solution.py:24
  89.2 1.2 reshape.483
  91.6 1.5 copy.16
  93.0 2.8 %select_n.381 = bf16[1024,288]{0,1:T(8,128)(2,1)} reshape(bf16[2,2,2,128,288]{3,2,1,0,4:T(2,128)(2,1)} %copy.16) | data formatting | bytes 1179648 | tf_op jit(solution)/shard_map/jit(_where)/select_n | solution.py:81
  98.5 2.0 multiply_convert_fusion.8
  100.5 1.2 copy.35
  101.8 1.4 fusion.45
  104.1 1.4 fusion.7
  108.3 2.3 %collective-permute-start.26 = (f32[8,128]{1,0:T(8,128)S(1)}, f32[8,128]{1,0:T(8,128)S(1)}, u32[]{:S(2)}, u32[]{:S(2)}) collective-permute-start(f32[8,128]{1,0:T(8,128)S(1)} %bitcast.251), channel_id=1, source_target_pairs={{0,28},{4,24},{8,20},{12,16},{16,12},{20,8},{24,4},{28,0},{1,29},{... | collective-permute-start | bytes 12296 | tf_op jit(solution)/shard_map/ppermute | solution.py:62
  110.6 1.9 collective-permute-start.25
  112.5 3.5 %collective-permute-start.23 = (f32[8,128]{1,0:T(8,128)S(1)}, f32[8,128]{1,0:T(8,128)S(1)}, u32[]{:S(2)}, u32[]{:S(2)}) collective-permute-start(f32[8,128]{1,0:T(8,128)S(1)} %bitcast.254), channel_id=1, source_target_pairs={{0,16},{4,20},{8,24},{12,28},{16,0},{20,4},{24,8},{28,12},{1,17},{... | collective-permute-start | bytes 12296 | tf_op jit(solution)/shard_map/ppermute | solution.py:62
  116.9 2.6 %collective-permute-start.21 = (f32[8,128]{1,0:T(8,128)S(1)}, f32[8,128]{1,0:T(8,128)S(1)}, u32[]{:S(2)}, u32[]{:S(2)}) collective-permute-start(f32[8,128]{1,0:T(8,128)S(1)} %bitcast.257), channel_id=1, source_target_pairs={{0,8},{4,12},{8,0},{12,4},{16,24},{20,28},{24,16},{28,20},{1,9},{5... | collective-permute-start | bytes 12296 | tf_op jit(solution)/shard_map/ppermute | solution.py:62
  121.1 1.6 multiply_convert_fusion.4
  123.6 1.4 pad_maximum_fusion
  126.0 1.4 pad_maximum_fusion.1
  132.7 1.8 maximum_add_fusion
  134.6 3.0 %maximum_add_fusion.1 = f32[2,1024,384]{2,1,0:T(8,128)S(1)} fusion(f32[1,1024,384]{2,1,0:T(8,128)S(1)} %convolution_bitcast_fusion, f32[1,1024,384]{2,1,0:T(8,128)S(1)} %convolution_bitcast_fusion.1, bf16[2,1024,384]{2,1,0:T(8,128)(2,1)} %collective-permute-done.28), kind=kLoop, calls=%fused_computation.2 | loop fusion | flops 2359296 | bytes 7864320 | tf_op jit(solution)/shard_map/add | solution.py:171
  138.7 1.7 maximum_add_fusion.2
  140.5 1.4 copy-done.5
  141.9 1.6 collective-permute-start.30
  144.4 2.0 collective-permute-start.32
  146.4 12.0 %collective-permute-done.32 = bf16[2,2,2,128,256]{4,3,2,0,1:T(8,128)(2,1)} collective-permute-done((bf16[2,2,2,128,256]{4,3,2,0,1:T(8,128)(2,1)S(1)}, bf16[2,2,2,128,256]{4,3,2,0,1:T(8,128)(2,1)}, u32[]{:S(2)}, u32[]{:S(2)}) %collective-permute-start.32) | collective-permute-done | bytes 524320 | tf_op jit(solution)/shard_map/ppermute | solution.py:62
  158.4 3.5 %collective-permute-done.30 = bf16[2,2,2,128,384]{4,3,0,1,2:T(8,128)(2,1)} collective-permute-done((bf16[2,2,2,128,384]{4,3,0,1,2:T(8,128)(2,1)S(1)}, bf16[2,2,2,128,384]{4,3,0,1,2:T(8,128)(2,1)}, u32[]{:S(2)}, u32[]{:S(2)}) %collective-permute-start.30) | collective-permute-done | bytes 786464 | tf_op jit(solution)/shard_map/ppermute | solution.py:62
  161.9 1.4 collective-permute-done.31
  163.3 1.8 bitcast_add_fusion.1
  165.1 1.2 copy-done.9
  166.4 1.5 bitcast_add_fusion
  171.6 2.0 collective-permute-start.34
  174.1 13.0 %collective-permute-done.35 = bf16[2,2,128,256]{3,2,1,0:T(8,128)(2,1)} collective-permute-done((bf16[2,2,128,256]{3,2,1,0:T(8,128)(2,1)}, bf16[2,2,128,256]{3,2,1,0:T(8,128)(2,1)}, u32[]{:S(2)}, u32[]{:S(2)}) %collective-permute-start.35) | collective-permute-done | bytes 262176 | tf_op jit(solution)/shard_map/ppermute | solution.py:62
  187.8 1.3 bitcast_add_fusion.4
  191.3 2.3 %collective-permute-start.36 = (bf16[2,128,384]{2,1,0:T(8,128)(2,1)S(1)}, bf16[2,128,384]{2,1,0:T(8,128)(2,1)S(1)}, u32[]{:S(2)}, u32[]{:S(2)}) collective-permute-start(bf16[2,128,384]{2,1,0:T(8,128)(2,1)S(1)} %fusion.67), channel_id=1, source_target_pairs={{0,8},{4,12},{8,0},{12,4},{16,24},{20,28},{24,16},{28,20},{1,9},{5... | collective-permute-start | bytes 589832 | tf_op jit(solution)/shard_map/ppermute | solution.py:62
  194.6 4.4 %collective-permute-done.38 = bf16[2,128,256]{2,1,0:T(8,128)(2,1)S(1)} collective-permute-done((bf16[2,128,256]{2,1,0:T(8,128)(2,1)S(1)}, bf16[2,128,256]{2,1,0:T(8,128)(2,1)S(1)}, u32[]{:S(2)}, u32[]{:S(2)}) %collective-permute-start.38) | collective-permute-done | bytes 131104 | tf_op jit(solution)/shard_map/ppermute | solution.py:62
  199.5 5.1 %collective-permute-done.37 = bf16[2,128,384]{2,1,0:T(8,128)(2,1)S(1)} collective-permute-done((bf16[2,128,384]{2,1,0:T(8,128)(2,1)S(1)}, bf16[2,128,384]{2,1,0:T(8,128)(2,1)S(1)}, u32[]{:S(2)}, u32[]{:S(2)}) %collective-permute-start.37) | collective-permute-done | bytes 196640 | tf_op jit(solution)/shard_map/ppermute | solution.py:62
  205.5 4.3 %collective-permute-done.41 = bf16[128,256]{1,0:T(8,128)(2,1)S(1)} collective-permute-done((bf16[128,256]{1,0:T(8,128)(2,1)S(1)}, bf16[128,256]{1,0:T(8,128)(2,1)S(1)}, u32[]{:S(2)}, u32[]{:S(2)}) %collective-permute-start.41) | collective-permute-done | bytes 65568 | tf_op jit(solution)/shard_map/ppermute | solution.py:62
  (192 shorter events, 40.2 us)
Async XLA Ops:
  0.0 122.7 %copy-start = (bf16[1,256,4096]{2,1,0:T(8,128)(2,1)S(1)}, bf16[1,256,4096]{2,1,0:T(8,128)(2,1)}, u32[]{:S(2)}) copy-start(bf16[1,256,4096]{2,1,0:T(8,128)(2,1)} %param.13) | copy-start | bytes 6291460
  1.7 68.4 %collective-permute-start = (bf16[128,288]{0,1:T(8,128)(2,1)}, bf16[128,288]{0,1:T(8,128)(2,1)S(1)}, u32[]{:S(2)}, u32[]{:S(2)}) collective-permute-start(bf16[128,288]{0,1:T(8,128)(2,1)} %get-tuple-element.66), channel_id=1, source_target_pairs={{0,16},{4,20},{8,24},{12,28},{16,0},{20,4},{24,8},{28,12},{1,17},{... | collective-permute-start | bytes 221192 | tf_op jit(solution)/shard_map/ppermute | solution.py:62
  7.3 13.0 %collective-permute-start.3 = (bf16[128,256]{0,1:T(8,128)(2,1)}, bf16[128,256]{0,1:T(8,128)(2,1)S(1)}, u32[]{:S(2)}, u32[]{:S(2)}) collective-permute-start(bf16[128,256]{0,1:T(8,128)(2,1)} %get-tuple-element.63), channel_id=1, source_target_pairs={{0,16},{4,20},{8,24},{12,28},{16,0},{20,4},{24,8},{28,12},{1,17},{... | collective-permute-start | bytes 196616 | tf_op jit(solution)/shard_map/ppermute | solution.py:62
  11.3 12.6 %collective-permute-start.13 = (bf16[128,256]{0,1:T(8,128)(2,1)}, bf16[128,256]{0,1:T(8,128)(2,1)}, u32[]{:S(2)}, u32[]{:S(2)}) collective-permute-start(bf16[128,256]{0,1:T(8,128)(2,1)} %get-tuple-element.76), channel_id=1, source_target_pairs={{0,4},{4,0},{8,12},{12,8},{16,20},{20,16},{24,28},{28,24},{1,5},{5... | collective-permute-start | bytes 196616 | tf_op jit(solution)/shard_map/ppermute | solution.py:62
  13.2 16.3 %collective-permute-start.14 = (bf16[128,256]{0,1:T(8,128)(2,1)}, bf16[128,256]{0,1:T(8,128)(2,1)}, u32[]{:S(2)}, u32[]{:S(2)}) collective-permute-start(bf16[128,256]{0,1:T(8,128)(2,1)} %get-tuple-element.75), channel_id=1, source_target_pairs={{0,8},{4,12},{8,0},{12,4},{16,24},{20,28},{24,16},{28,20},{1,9},{5... | collective-permute-start | bytes 196616 | tf_op jit(solution)/shard_map/ppermute | solution.py:62
  14.7 23.8 %collective-permute-start.15 = (bf16[128,256]{0,1:T(8,128)(2,1)}, bf16[128,256]{0,1:T(8,128)(2,1)S(1)}, u32[]{:S(2)}, u32[]{:S(2)}) collective-permute-start(bf16[128,256]{0,1:T(8,128)(2,1)} %get-tuple-element.74), channel_id=1, source_target_pairs={{0,12},{4,8},{8,4},{12,0},{16,28},{20,24},{24,20},{28,16},{1,13},{... | collective-permute-start | bytes 196616 | tf_op jit(solution)/shard_map/ppermute | solution.py:62
  16.8 17.0 %copy-start.15 = (bf16[128,256]{0,1:T(8,128)(2,1)S(1)}, bf16[128,256]{0,1:T(8,128)(2,1)}, u32[]{:S(2)}) copy-start(bf16[128,256]{0,1:T(8,128)(2,1)} %get-tuple-element.71) | copy-start | bytes 196612
  16.8 27.1 %copy-start.14 = (bf16[128,256]{0,1:T(8,128)(2,1)S(1)}, bf16[128,256]{0,1:T(8,128)(2,1)}, u32[]{:S(2)}) copy-start(bf16[128,256]{0,1:T(8,128)(2,1)} %get-tuple-element.70) | copy-start | bytes 196612
  16.9 50.8 %copy-start.18 = (f32[1,256]{1,0:T(1,128)S(1)}, f32[1,256]{1,0:T(1,128)}, u32[]{:S(2)}) copy-start(f32[1,256]{1,0:T(1,128)} %get-tuple-element.100) | copy-start | bytes 3076
  20.3 24.2 %collective-permute-start.16 = (bf16[128,256]{0,1:T(8,128)(2,1)}, bf16[128,256]{0,1:T(8,128)(2,1)S(1)}, u32[]{:S(2)}, u32[]{:S(2)}) collective-permute-start(bf16[128,256]{0,1:T(8,128)(2,1)} %get-tuple-element.73), channel_id=1, source_target_pairs={{0,16},{4,20},{8,24},{12,28},{16,0},{20,4},{24,8},{28,12},{1,17},{... | collective-permute-start | bytes 196616 | tf_op jit(solution)/shard_map/ppermute | solution.py:62
  23.9 4.3 %collective-permute-start.6 = (bf16[128,256]{0,1:T(8,128)(2,1)S(1)}, bf16[128,256]{0,1:T(8,128)(2,1)S(1)}, u32[]{:S(2)}, u32[]{:S(2)}) collective-permute-start(bf16[128,256]{0,1:T(8,128)(2,1)S(1)} %get-tuple-element.84), channel_id=1, source_target_pairs={{0,4},{4,0},{8,12},{12,8},{16,20},{20,16},{24,28},{28,24},{1,5},{5... | collective-permute-start | bytes 196616 | tf_op jit(solution)/shard_map/ppermute | solution.py:62
  28.1 25.0 %collective-permute-start.17 = (bf16[128,256]{0,1:T(8,128)(2,1)}, bf16[128,256]{0,1:T(8,128)(2,1)S(1)}, u32[]{:S(2)}, u32[]{:S(2)}) collective-permute-start(bf16[128,256]{0,1:T(8,128)(2,1)} %get-tuple-element.72), channel_id=1, source_target_pairs={{0,20},{4,16},{8,28},{12,24},{16,4},{20,0},{24,12},{28,8},{1,21},{... | collective-permute-start | bytes 196616 | tf_op jit(solution)/shard_map/ppermute | solution.py:62
  29.5 4.3 %collective-permute-start.7 = (bf16[128,256]{0,1:T(8,128)(2,1)S(1)}, bf16[128,256]{0,1:T(8,128)(2,1)S(1)}, u32[]{:S(2)}, u32[]{:S(2)}) collective-permute-start(bf16[128,256]{0,1:T(8,128)(2,1)S(1)} %get-tuple-element.83), channel_id=1, source_target_pairs={{0,8},{4,12},{8,0},{12,4},{16,24},{20,28},{24,16},{28,20},{1,9},{5... | collective-permute-start | bytes 196616 | tf_op jit(solution)/shard_map/ppermute | solution.py:62
  33.8 28.4 %collective-permute-start.18 = (bf16[128,256]{0,1:T(8,128)(2,1)S(1)}, bf16[128,256]{0,1:T(8,128)(2,1)S(1)}, u32[]{:S(2)}, u32[]{:S(2)}) collective-permute-start(bf16[128,256]{0,1:T(8,128)(2,1)S(1)} %copy-done.15), channel_id=1, source_target_pairs={{0,24},{4,28},{8,16},{12,20},{16,8},{20,12},{24,0},{28,4},{1,25},{... | collective-permute-start | bytes 196616 | tf_op jit(solution)/shard_map/ppermute | solution.py:62
  38.5 5.3 %collective-permute-start.8 = (bf16[128,256]{0,1:T(8,128)(2,1)S(1)}, bf16[128,256]{0,1:T(8,128)(2,1)S(1)}, u32[]{:S(2)}, u32[]{:S(2)}) collective-permute-start(bf16[128,256]{0,1:T(8,128)(2,1)S(1)} %get-tuple-element.82), channel_id=1, source_target_pairs={{0,12},{4,8},{8,4},{12,0},{16,28},{20,24},{24,20},{28,16},{1,13},{... | collective-permute-start | bytes 196616 | tf_op jit(solution)/shard_map/ppermute | solution.py:62
  43.9 18.4 %collective-permute-start.19 = (bf16[128,256]{0,1:T(8,128)(2,1)S(1)}, bf16[128,256]{0,1:T(8,128)(2,1)S(1)}, u32[]{:S(2)}, u32[]{:S(2)}) collective-permute-start(bf16[128,256]{0,1:T(8,128)(2,1)S(1)} %copy-done.14), channel_id=1, source_target_pairs={{0,28},{4,24},{8,20},{12,16},{16,12},{20,8},{24,4},{28,0},{1,29},{... | collective-permute-start | bytes 196616 | tf_op jit(solution)/shard_map/ppermute | solution.py:62
  44.5 8.5 %collective-permute-start.9 = (bf16[128,256]{0,1:T(8,128)(2,1)S(1)}, bf16[128,256]{0,1:T(8,128)(2,1)S(1)}, u32[]{:S(2)}, u32[]{:S(2)}) collective-permute-start(bf16[128,256]{0,1:T(8,128)(2,1)S(1)} %get-tuple-element.81), channel_id=1, source_target_pairs={{0,16},{4,20},{8,24},{12,28},{16,0},{20,4},{24,8},{28,12},{1,17},{... | collective-permute-start | bytes 196616 | tf_op jit(solution)/shard_map/ppermute | solution.py:62
  53.0 6.9 %collective-permute-start.10 = (bf16[128,256]{0,1:T(8,128)(2,1)S(1)}, bf16[128,256]{0,1:T(8,128)(2,1)S(1)}, u32[]{:S(2)}, u32[]{:S(2)}) collective-permute-start(bf16[128,256]{0,1:T(8,128)(2,1)S(1)} %get-tuple-element.80), channel_id=1, source_target_pairs={{0,20},{4,16},{8,28},{12,24},{16,4},{20,0},{24,12},{28,8},{1,21},{... | collective-permute-start | bytes 196616 | tf_op jit(solution)/shard_map/ppermute | solution.py:62
  53.1 9.2 %collective-permute-start.11 = (bf16[128,256]{0,1:T(8,128)(2,1)S(1)}, bf16[128,256]{0,1:T(8,128)(2,1)S(1)}, u32[]{:S(2)}, u32[]{:S(2)}) collective-permute-start(bf16[128,256]{0,1:T(8,128)(2,1)S(1)} %get-tuple-element.79), channel_id=1, source_target_pairs={{0,24},{4,28},{8,16},{12,20},{16,8},{20,12},{24,0},{28,4},{1,25},{... | collective-permute-start | bytes 196616 | tf_op jit(solution)/shard_map/ppermute | solution.py:62
  59.9 7.7 %collective-permute-start.12 = (bf16[128,256]{0,1:T(8,128)(2,1)S(1)}, bf16[128,256]{0,1:T(8,128)(2,1)S(1)}, u32[]{:S(2)}, u32[]{:S(2)}) collective-permute-start(bf16[128,256]{0,1:T(8,128)(2,1)S(1)} %get-tuple-element.78), channel_id=1, source_target_pairs={{0,28},{4,24},{8,20},{12,16},{16,12},{20,8},{24,4},{28,0},{1,29},{... | collective-permute-start | bytes 196616 | tf_op jit(solution)/shard_map/ppermute | solution.py:62
  62.2 9.1 %collective-permute-start.4 = (bf16[2,128,256]{1,2,0:T(8,128)(2,1)}, bf16[2,128,256]{1,2,0:T(8,128)(2,1)S(1)}, u32[]{:S(2)}, u32[]{:S(2)}) collective-permute-start(bf16[2,128,256]{1,2,0:T(8,128)(2,1)} %maximum_select_fusion.9), channel_id=1, source_target_pairs={{0,4},{4,0},{8,12},{12,8},{16,20},{20,16},{24,28},{28,24},{1,5},{5... | collective-permute-start | bytes 393224 | tf_op jit(solution)/shard_map/ppermute | solution.py:62
  71.2 5.2 %collective-permute-start.1 = (bf16[2,128,288]{1,2,0:T(8,128)(2,1)S(1)}, bf16[2,128,288]{1,2,0:T(8,128)(2,1)S(1)}, u32[]{:S(2)}, u32[]{:S(2)}) collective-permute-start(bf16[2,128,288]{1,2,0:T(8,128)(2,1)S(1)} %maximum_select_fusion.7), channel_id=1, source_target_pairs={{0,8},{4,12},{8,0},{12,4},{16,24},{20,28},{24,16},{28,20},{1,9},{5... | collective-permute-start | bytes 442376 | tf_op jit(solution)/shard_map/ppermute | solution.py:62
  71.3 7.8 %collective-permute-start.5 = (bf16[2,2,128,256]{2,3,0,1:T(8,128)(2,1)S(1)}, bf16[2,2,128,256]{2,3,0,1:T(8,128)(2,1)S(1)}, u32[]{:S(2)}, u32[]{:S(2)}) collective-permute-start(bf16[2,2,128,256]{2,3,0,1:T(8,128)(2,1)S(1)} %maximum_select_fusion.5), channel_id=1, source_target_pairs={{0,8},{4,12},{8,0},{12,4},{16,24},{20,28},{24,16},{28,20},{1,9},{5... | collective-permute-start | bytes 786440 | tf_op jit(solution)/shard_map/ppermute | solution.py:62
  77.1 13.3 %collective-permute-start.2 = (bf16[2,2,128,288]{2,3,0,1:T(8,128)(2,1)}, bf16[2,2,128,288]{2,3,0,1:T(8,128)(2,1)}, u32[]{:S(2)}, u32[]{:S(2)}) collective-permute-start(bf16[2,2,128,288]{2,3,0,1:T(8,128)(2,1)} %maximum_select_fusion.3), channel_id=1, source_target_pairs={{0,4},{4,0},{8,12},{12,8},{16,20},{20,16},{24,28},{28,24},{1,5},{5... | collective-permute-start | bytes 884744 | tf_op jit(solution)/shard_map/ppermute | solution.py:62
  80.3 5.1 %copy-start.17 = (f32[1,256]{1,0:T(1,128)S(1)}, f32[1,256]{1,0:T(1,128)}, u32[]{:S(2)}) copy-start(f32[1,256]{1,0:T(1,128)} %get-tuple-element.102) | copy-start | bytes 3076
  80.3 5.1 %copy-start.23 = (f32[1,1,256]{2,1,0:T(1,128)S(1)}, f32[1,1,256]{2,1,0:T(1,128)}, u32[]{:S(2)}) copy-start(f32[1,1,256]{2,1,0:T(1,128)} %get-tuple-element.89) | copy-start | bytes 3076
  80.3 5.1 %copy-start.24 = (f32[1,1,256]{2,1,0:T(1,128)S(1)}, f32[1,1,256]{2,1,0:T(1,128)}, u32[]{:S(2)}) copy-start(f32[1,1,256]{2,1,0:T(1,128)} %get-tuple-element.90) | copy-start | bytes 3076
  80.3 5.1 %copy-start.25 = (f32[1,1,256]{2,1,0:T(1,128)S(1)}, f32[1,1,256]{2,1,0:T(1,128)}, u32[]{:S(2)}) copy-start(f32[1,1,256]{2,1,0:T(1,128)} %get-tuple-element.91) | copy-start | bytes 3076
  80.3 5.1 %copy-start.26 = (f32[1,1,256]{2,1,0:T(1,128)S(1)}, f32[1,1,256]{2,1,0:T(1,128)}, u32[]{:S(2)}) copy-start(f32[1,1,256]{2,1,0:T(1,128)} %get-tuple-element.97) | copy-start | bytes 3076
  89.2 6.6 %copy-start.10 = (bf16[1024,256]{0,1:T(8,128)(2,1)}, bf16[1024,256]{0,1:T(8,128)(2,1)S(1)}, u32[]{:S(2)}) copy-start(bf16[1024,256]{0,1:T(8,128)(2,1)S(1)} %multiply_convert_fusion.7) | copy-start | bytes 1572868
  91.5 6.3 %copy-start.27 = (f32[4]{0:T(128)S(1)}, f32[4]{0:T(128)}, u32[]{:S(2)}) copy-start(f32[4]{0:T(128)} %get-tuple-element.106) | copy-start | bytes 52
  91.5 6.4 %copy-start.29 = (f32[4]{0:T(128)S(1)}, f32[4]{0:T(128)}, u32[]{:S(2)}) copy-start(f32[4]{0:T(128)} %get-tuple-element.107) | copy-start | bytes 52
  91.5 6.9 %copy-start.16 = (f32[1,256]{1,0:T(1,128)S(1)}, f32[1,256]{1,0:T(1,128)}, u32[]{:S(2)}) copy-start(f32[1,256]{1,0:T(1,128)} %get-tuple-element.101) | copy-start | bytes 3076
  91.5 6.9 %copy-start.19 = (f32[1,1,256]{2,1,0:T(1,128)S(1)}, f32[1,1,256]{2,1,0:T(1,128)}, u32[]{:S(2)}) copy-start(f32[1,1,256]{2,1,0:T(1,128)} %get-tuple-element.92) | copy-start | bytes 3076
  91.6 6.9 %copy-start.20 = (f32[1,1,256]{2,1,0:T(1,128)S(1)}, f32[1,1,256]{2,1,0:T(1,128)}, u32[]{:S(2)}) copy-start(f32[1,1,256]{2,1,0:T(1,128)} %get-tuple-element.93) | copy-start | bytes 3076
  91.6 6.9 %copy-start.21 = (f32[1,1,256]{2,1,0:T(1,128)S(1)}, f32[1,1,256]{2,1,0:T(1,128)}, u32[]{:S(2)}) copy-start(f32[1,1,256]{2,1,0:T(1,128)} %get-tuple-element.94) | copy-start | bytes 3076
  91.6 6.9 %copy-start.22 = (f32[1,1,256]{2,1,0:T(1,128)S(1)}, f32[1,1,256]{2,1,0:T(1,128)}, u32[]{:S(2)}) copy-start(f32[1,1,256]{2,1,0:T(1,128)} %get-tuple-element.95) | copy-start | bytes 3076
  108.3 7.7 %collective-permute-start.26 = (f32[8,128]{1,0:T(8,128)S(1)}, f32[8,128]{1,0:T(8,128)S(1)}, u32[]{:S(2)}, u32[]{:S(2)}) collective-permute-start(f32[8,128]{1,0:T(8,128)S(1)} %bitcast.251), channel_id=1, source_target_pairs={{0,28},{4,24},{8,20},{12,16},{16,12},{20,8},{24,4},{28,0},{1,29},{... | collective-permute-start | bytes 12296 | tf_op jit(solution)/shard_map/ppermute | solution.py:62
  110.6 6.3 %collective-permute-start.25 = (f32[8,128]{1,0:T(8,128)S(1)}, f32[8,128]{1,0:T(8,128)S(1)}, u32[]{:S(2)}, u32[]{:S(2)}) collective-permute-start(f32[8,128]{1,0:T(8,128)S(1)} %bitcast.252), channel_id=1, source_target_pairs={{0,24},{4,28},{8,16},{12,20},{16,8},{20,12},{24,0},{28,4},{1,25},{... | collective-permute-start | bytes 12296 | tf_op jit(solution)/shard_map/ppermute | solution.py:62
  112.5 7.7 %collective-permute-start.24 = (f32[8,128]{1,0:T(8,128)S(1)}, f32[8,128]{1,0:T(8,128)S(1)}, u32[]{:S(2)}, u32[]{:S(2)}) collective-permute-start(f32[8,128]{1,0:T(8,128)S(1)} %bitcast.253), channel_id=1, source_target_pairs={{0,20},{4,16},{8,28},{12,24},{16,4},{20,0},{24,12},{28,8},{1,21},{... | collective-permute-start | bytes 12296 | tf_op jit(solution)/shard_map/ppermute | solution.py:62
  112.5 7.7 %collective-permute-start.23 = (f32[8,128]{1,0:T(8,128)S(1)}, f32[8,128]{1,0:T(8,128)S(1)}, u32[]{:S(2)}, u32[]{:S(2)}) collective-permute-start(f32[8,128]{1,0:T(8,128)S(1)} %bitcast.254), channel_id=1, source_target_pairs={{0,16},{4,20},{8,24},{12,28},{16,0},{20,4},{24,8},{28,12},{1,17},{... | collective-permute-start | bytes 12296 | tf_op jit(solution)/shard_map/ppermute | solution.py:62
  116.0 4.5 %collective-permute-start.22 = (f32[8,128]{1,0:T(8,128)S(1)}, f32[8,128]{1,0:T(8,128)S(1)}, u32[]{:S(2)}, u32[]{:S(2)}) collective-permute-start(f32[8,128]{1,0:T(8,128)S(1)} %bitcast.255), channel_id=1, source_target_pairs={{0,12},{4,8},{8,4},{12,0},{16,28},{20,24},{24,20},{28,16},{1,13},{... | collective-permute-start | bytes 12296 | tf_op jit(solution)/shard_map/ppermute | solution.py:62
  116.0 4.5 %collective-permute-start.20 = (f32[8,128]{1,0:T(8,128)S(1)}, f32[8,128]{1,0:T(8,128)S(1)}, u32[]{:S(2)}, u32[]{:S(2)}) collective-permute-start(f32[8,128]{1,0:T(8,128)S(1)} %bitcast.256), channel_id=1, source_target_pairs={{0,4},{4,0},{8,12},{12,8},{16,20},{20,16},{24,28},{28,24},{1,5},{5... | collective-permute-start | bytes 12296 | tf_op jit(solution)/shard_map/ppermute | solution.py:62
  116.9 4.2 %collective-permute-start.21 = (f32[8,128]{1,0:T(8,128)S(1)}, f32[8,128]{1,0:T(8,128)S(1)}, u32[]{:S(2)}, u32[]{:S(2)}) collective-permute-start(f32[8,128]{1,0:T(8,128)S(1)} %bitcast.257), channel_id=1, source_target_pairs={{0,8},{4,12},{8,0},{12,4},{16,24},{20,28},{24,16},{28,20},{1,9},{5... | collective-permute-start | bytes 12296 | tf_op jit(solution)/shard_map/ppermute | solution.py:62
  125.0 7.7 %collective-permute-start.27 = (bf16[2,1024,384]{2,1,0:T(8,128)(2,1)}, bf16[2,1024,384]{2,1,0:T(8,128)(2,1)}, u32[]{:S(2)}, u32[]{:S(2)}) collective-permute-start(bf16[2,1024,384]{2,1,0:T(8,128)(2,1)} %pad_maximum_fusion), channel_id=1, source_target_pairs={{0,1},{1,0},{2,3},{3,2},{4,5},{5,4},{6,7},{7,6},{8,9},{9,8},{10,11... | collective-permute-start | bytes 4718600 | tf_op jit(solution)/shard_map/ppermute | solution.py:62
  127.3 5.4 %collective-permute-start.28 = (bf16[2,1024,384]{2,1,0:T(8,128)(2,1)}, bf16[2,1024,384]{2,1,0:T(8,128)(2,1)}, u32[]{:S(2)}, u32[]{:S(2)}) collective-permute-start(bf16[2,1024,384]{2,1,0:T(8,128)(2,1)} %pad_maximum_fusion.1), channel_id=1, source_target_pairs={{0,1},{1,0},{2,3},{3,2},{4,5},{5,4},{6,7},{7,6},{8,9},{9,8},{10,11... | collective-permute-start | bytes 4718600 | tf_op jit(solution)/shard_map/ppermute | solution.py:62
  129.7 3.0 %collective-permute-start.29 = (bf16[2,1024,256]{2,1,0:T(8,128)(2,1)}, bf16[2,1024,256]{2,1,0:T(8,128)(2,1)}, u32[]{:S(2)}, u32[]{:S(2)}) collective-permute-start(bf16[2,1024,256]{2,1,0:T(8,128)(2,1)} %pad_maximum_fusion.2), channel_id=1, source_target_pairs={{0,1},{1,0},{2,3},{3,2},{4,5},{5,4},{6,7},{7,6},{8,9},{9,8},{10,11... | collective-permute-start | bytes 3145736 | tf_op jit(solution)/shard_map/ppermute | solution.py:62
  134.5 3.1 %copy-start.1 = (f32[2,1024,384]{2,1,0:T(8,128)}, f32[2,1024,384]{2,1,0:T(8,128)S(1)}, u32[]{:S(2)}) copy-start(f32[2,1024,384]{2,1,0:T(8,128)S(1)} %maximum_add_fusion) | copy-start | bytes 9437188
  137.6 2.8 %copy-start.2 = (f32[2,1024,384]{2,1,0:T(8,128)}, f32[2,1024,384]{2,1,0:T(8,128)S(1)}, u32[]{:S(2)}) copy-start(f32[2,1024,384]{2,1,0:T(8,128)S(1)} %maximum_add_fusion.1) | copy-start | bytes 9437188
  141.9 20.0 %collective-permute-start.30 = (bf16[2,2,2,128,384]{4,3,0,1,2:T(8,128)(2,1)S(1)}, bf16[2,2,2,128,384]{4,3,0,1,2:T(8,128)(2,1)}, u32[]{:S(2)}, u32[]{:S(2)}) collective-permute-start(bf16[2,2,2,128,384]{4,3,0,1,2:T(8,128)(2,1)S(1)} %fusion.42), channel_id=1, source_target_pairs={{0,2},{1,3},{2,0},{3,1},{4,6},{5,7},{6,4},{7,5},{8,10},{9,11},{10,... | collective-permute-start | bytes 2359304 | tf_op jit(solution)/shard_map/ppermute | solution.py:62
  143.5 19.8 %collective-permute-start.31 = (bf16[2,2,2,128,384]{4,3,0,1,2:T(8,128)(2,1)}, bf16[2,2,2,128,384]{4,3,0,1,2:T(8,128)(2,1)}, u32[]{:S(2)}, u32[]{:S(2)}) collective-permute-start(bf16[2,2,2,128,384]{4,3,0,1,2:T(8,128)(2,1)} %fusion.43), channel_id=1, source_target_pairs={{0,4},{4,0},{8,12},{12,8},{16,20},{20,16},{24,28},{28,24},{1,5},{5... | collective-permute-start | bytes 2359304 | tf_op jit(solution)/shard_map/ppermute | solution.py:62
  144.4 14.0 %collective-permute-start.32 = (bf16[2,2,2,128,256]{4,3,2,0,1:T(8,128)(2,1)S(1)}, bf16[2,2,2,128,256]{4,3,2,0,1:T(8,128)(2,1)}, u32[]{:S(2)}, u32[]{:S(2)}) collective-permute-start(bf16[2,2,2,128,256]{4,3,2,0,1:T(8,128)(2,1)S(1)} %fusion.44), channel_id=1, source_target_pairs={{0,8},{4,12},{8,0},{12,4},{16,24},{20,28},{24,16},{28,20},{1,9},{5... | collective-permute-start | bytes 1572872 | tf_op jit(solution)/shard_map/ppermute | solution.py:62
  146.4 20.0 %copy-start.3 = (f32[2,1024,384]{2,1,0:T(8,128)S(1)}, f32[2,1024,384]{2,1,0:T(8,128)}, u32[]{:S(2)}) copy-start(f32[2,1024,384]{2,1,0:T(8,128)} %copy-done.2) | copy-start | bytes 9437188
  166.4 2.4 %copy-start.6 = (f32[2,1024,256]{2,1,0:T(8,128)S(1)}, f32[2,1024,256]{2,1,0:T(8,128)}, u32[]{:S(2)}) copy-start(f32[2,1024,256]{2,1,0:T(8,128)} %copy-done.5) | copy-start | bytes 6291460
  170.7 16.3 %collective-permute-start.33 = (bf16[2,2,128,384]{3,2,0,1:T(8,128)(2,1)S(1)}, bf16[2,2,128,384]{3,2,0,1:T(8,128)(2,1)}, u32[]{:S(2)}, u32[]{:S(2)}) collective-permute-start(bf16[2,2,128,384]{3,2,0,1:T(8,128)(2,1)S(1)} %fusion.59), channel_id=1, source_target_pairs={{0,4},{4,0},{8,12},{12,8},{16,20},{20,16},{24,28},{28,24},{1,5},{5... | collective-permute-start | bytes 1179656 | tf_op jit(solution)/shard_map/ppermute | solution.py:62
  171.6 16.2 %collective-permute-start.34 = (bf16[2,2,128,384]{3,2,0,1:T(8,128)(2,1)}, bf16[2,2,128,384]{3,2,0,1:T(8,128)(2,1)}, u32[]{:S(2)}, u32[]{:S(2)}) collective-permute-start(bf16[2,2,128,384]{3,2,0,1:T(8,128)(2,1)} %fusion.60), channel_id=1, source_target_pairs={{0,8},{4,12},{8,0},{12,4},{16,24},{20,28},{24,16},{28,20},{1,9},{5... | collective-permute-start | bytes 1179656 | tf_op jit(solution)/shard_map/ppermute | solution.py:62
  173.6 13.4 %collective-permute-start.35 = (bf16[2,2,128,256]{3,2,1,0:T(8,128)(2,1)}, bf16[2,2,128,256]{3,2,1,0:T(8,128)(2,1)}, u32[]{:S(2)}, u32[]{:S(2)}) collective-permute-start(bf16[2,2,128,256]{3,2,1,0:T(8,128)(2,1)} %fusion.61), channel_id=1, source_target_pairs={{0,16},{4,20},{8,24},{12,28},{16,0},{20,4},{24,8},{28,12},{1,17},{... | collective-permute-start | bytes 786440 | tf_op jit(solution)/shard_map/ppermute | solution.py:62
  174.1 15.1 %copy-start.8 = (f32[2,2,2,128,384]{4,3,0,1,2:T(8,128)S(1)}, f32[2,2,2,128,384]{4,3,0,1,2:T(8,128)}, u32[]{:S(2)}) copy-start(f32[2,2,2,128,384]{4,3,0,1,2:T(8,128)} %copy-done.7) | copy-start | bytes 4718596
  191.3 8.2 %collective-permute-start.36 = (bf16[2,128,384]{2,1,0:T(8,128)(2,1)S(1)}, bf16[2,128,384]{2,1,0:T(8,128)(2,1)S(1)}, u32[]{:S(2)}, u32[]{:S(2)}) collective-permute-start(bf16[2,128,384]{2,1,0:T(8,128)(2,1)S(1)} %fusion.67), channel_id=1, source_target_pairs={{0,8},{4,12},{8,0},{12,4},{16,24},{20,28},{24,16},{28,20},{1,9},{5... | collective-permute-start | bytes 589832 | tf_op jit(solution)/shard_map/ppermute | solution.py:62
  193.6 11.1 %collective-permute-start.37 = (bf16[2,128,384]{2,1,0:T(8,128)(2,1)S(1)}, bf16[2,128,384]{2,1,0:T(8,128)(2,1)S(1)}, u32[]{:S(2)}, u32[]{:S(2)}) collective-permute-start(bf16[2,128,384]{2,1,0:T(8,128)(2,1)S(1)} %fusion.68), channel_id=1, source_target_pairs={{0,16},{4,20},{8,24},{12,28},{16,0},{20,4},{24,8},{28,12},{1,17},{... | collective-permute-start | bytes 589832 | tf_op jit(solution)/shard_map/ppermute | solution.py:62
  194.1 5.0 %collective-permute-start.38 = (bf16[2,128,256]{2,1,0:T(8,128)(2,1)S(1)}, bf16[2,128,256]{2,1,0:T(8,128)(2,1)S(1)}, u32[]{:S(2)}, u32[]{:S(2)}) collective-permute-start(bf16[2,128,256]{2,1,0:T(8,128)(2,1)S(1)} %fusion.87), channel_id=1, source_target_pairs={{0,2},{1,3},{2,0},{3,1},{4,6},{5,7},{6,4},{7,5},{8,10},{9,11},{10,... | collective-permute-start | bytes 393224 | tf_op jit(solution)/shard_map/ppermute | solution.py:62
  204.8 5.7 %collective-permute-start.39 = (bf16[128,384]{1,0:T(8,128)(2,1)S(1)}, bf16[128,384]{1,0:T(8,128)(2,1)S(1)}, u32[]{:S(2)}, u32[]{:S(2)}) collective-permute-start(bf16[128,384]{1,0:T(8,128)(2,1)S(1)} %fusion.97), channel_id=1, source_target_pairs={{0,16},{4,20},{8,24},{12,28},{16,0},{20,4},{24,8},{28,12},{1,17},{... | collective-permute-start | bytes 294920 | tf_op jit(solution)/shard_map/ppermute | solution.py:62
  204.9 5.6 %collective-permute-start.40 = (bf16[128,384]{1,0:T(8,128)(2,1)S(1)}, bf16[128,384]{1,0:T(8,128)(2,1)S(1)}, u32[]{:S(2)}, u32[]{:S(2)}) collective-permute-start(bf16[128,384]{1,0:T(8,128)(2,1)S(1)} %fusion.98), channel_id=1, source_target_pairs={{0,2},{1,3},{2,0},{3,1},{4,6},{5,7},{6,4},{7,5},{8,10},{9,11},{10,... | collective-permute-start | bytes 294920 | tf_op jit(solution)/shard_map/ppermute | solution.py:62
  205.5 4.3 %collective-permute-start.41 = (bf16[128,256]{1,0:T(8,128)(2,1)S(1)}, bf16[128,256]{1,0:T(8,128)(2,1)S(1)}, u32[]{:S(2)}, u32[]{:S(2)}) collective-permute-start(bf16[128,256]{1,0:T(8,128)(2,1)S(1)} %fusion.99), channel_id=1, source_target_pairs={{0,4},{4,0},{8,12},{12,8},{16,20},{20,16},{24,28},{28,24},{1,5},{5... | collective-permute-start | bytes 196616 | tf_op jit(solution)/shard_map/ppermute | solution.py:62
  (8 other events, 11.2 us)

commit v3 on v1

--- a/solution.py
+++ b/solution.py
@@ -79,6 +79,8 @@
     heads = max(1, width // P_SIZE)
     here = projected[:, 0]
 
+    tail_columns, here = lax.optimization_barrier((here[:, 2 * GCH :], here))
+    shared = lax.all_gather(tail_columns, "ctx", axis=0, tiled=True)
     parts = [
         jnp.concatenate(
             [here[:, d * width : (d + 1) * width], here[:, GCH + d * width : GCH + (d + 1) * width]], axis=1
@@ -88,7 +90,6 @@
     moved = lax.all_to_all(jnp.stack(parts), "ctx", split_axis=0, concat_axis=0, tiled=True)
     tokens = devices * rows
     moved = moved.reshape(tokens, 2 * width)
-    shared = lax.all_gather(here[:, 2 * GCH :], "ctx", axis=0, tiled=True)
 
     first = me * width
     values = causal_conv(
@@ -134,22 +135,35 @@
     unit = columns // 8
     sizes = [3 * unit, 3 * unit, 2 * unit]
     names = tp_bits[::-1] + ctx_bits[::-1]
-    results = []
-    low = 0
-    for order, size in zip(orders, sizes):
+    lows = [0, sizes[0], sizes[0] + sizes[1]]
+    left = [list(names) for _ in orders]
+
+    def halves(total, index, stage):
+        name = orders[index][stage]
+        dim = left[index].index(name)
+        left[index].remove(name)
+        side = my_bit(*name)
+        away = lax.dynamic_index_in_dim(total, 1 - side, dim, keepdims=False).astype(BF16)
+        return away, lax.dynamic_index_in_dim(total, side, dim, keepdims=False)
+
+    aways, stays = [], []
+    for index, (low, size) in enumerate(zip(lows, sizes)):
         arrived = exchange(product(1 - mine, low, size).astype(BF16), "tp", first_bit)
         total = product(mine, low, size) + arrived.astype(F32)
-        total = total.reshape((2,) * len(names) + (rows, size))
-        left = list(names)
-        for name in order:
-            dim = left.index(name)
-            side = my_bit(*name)
-            away = lax.dynamic_index_in_dim(total, 1 - side, dim, keepdims=False).astype(BF16)
-            stay = lax.dynamic_index_in_dim(total, side, dim, keepdims=False)
-            total = stay + exchange(away, *name).astype(F32)
-            left.remove(name)
+        away, stay = halves(total.reshape((2,) * len(names) + (rows, size)), index, 0)
+        aways.append(away)
+        stays.append(stay)
+    aways = lax.optimization_barrier(aways)
+    first_arrived = lax.optimization_barrier(
+        [exchange(away, *order[0]) for away, order in zip(aways, orders)]
+    )
+    results = []
+    for index, (stay, arrived) in enumerate(zip(stays, first_arrived)):
+        total = stay + arrived.astype(F32)
+        for stage in range(1, len(names)):
+            away, stay = halves(total, index, stage)
+            total = stay + exchange(away, *orders[index][stage]).astype(F32)
         results.append(total)
-        low += size
     return jnp.concatenate(results, axis=1).astype(BF16)
 
 

time: 190 us -> 188 us (0.989)
  waiting for transfers between devices: 104 us -> 97.3 us
  local copies, waits for them, and re-layouts: 21.4 us -> 25.4 us
    ppermute x18, waiting for transfers between devices: 64.5 us -> 56.2 us  [exchange(): return lax.ppermute(array, axis, [(i, i ^ bit) for i in range(peers)])]
    unnamed x22 -> x26, local copies, waits for them, and re-layouts: 0.74 us -> 4.77 us
  transfers between devices with their start and end apart: 20 -> 20, of which waited for: 12 -> 17; matrix products, arithmetic and copies ran while one was open for 12% -> 10% of each run, Pallas kernels for 0% -> 0%
where the time goes in v3:
time: 188 us; the launch traced here: 187 us
  waiting for transfers between devices  97.3 us (52%)
  local copies, waits for them, and re-layouts  25.4 us (14%)
  starting transfers between devices  21.9 us (12%)
  other arithmetic  20.9 us (11%)
  between operations  13.9 us (7%)
  matrix products  7.42 us (4%)
    ppermute x18, waiting for transfers between devices, exchange(): return lax.ppermute(array, axis, [(i, i ^ bit) for i in range(peers)])  56.2 us
    all_to_all x1, waiting for transfers between devices, on_device(): lax.all_to_all(jnp.stack(parts), 'ctx', split_axis=0, concat_axis=0, tile...  27.6 us
    ppermute x18, starting transfers between devices, exchange(): return lax.ppermute(array, axis, [(i, i ^ bit) for i in range(peers)])  14.6 us
    all_gather x1, waiting for transfers between devices, on_device(): shared = lax.all_gather(tail_columns, 'ctx', axis=0, tiled=True)  12.8 us
    all_to_all x1, starting transfers between devices, on_device(): lax.all_to_all(jnp.stack(parts), 'ctx', split_axis=0, concat_axis=0, tile...  7.28 us
    unnamed x26, local copies, waits for them, and re-layouts  4.77 us
    dot_general x12, matrix products, product(): pieces.append(jnp.dot(normed, block, preferred_element_type=F32))  4.73 us
    unnamed x7, other arithmetic  4.63 us
  transfers between devices with their start and end apart: 20, of which 17 were waited for; matrix products, arithmetic and copies ran while one was open for 10% of the time, Pallas kernels for 0%

profile of v3, /device:TPU:0, one launch (start us, length us, event | category | flops | bytes accessed | tf_op | source)
XLA Modules:
  0.0 186.8 jit_solution(6843560568036147062)
XLA Ops:
  6.5 1.7 slice.194
  8.3 1.3 fusion.119
  9.6 0.7 fusion.78
  10.3 0.7 fusion.79
  10.9 0.7 fusion.80
  11.6 0.7 fusion.81
  12.3 0.7 fusion.82
  12.9 0.7 fusion.83
  13.6 0.7 fusion.84
  14.2 0.7 fusion.85
  14.9 7.3 %all-to-all-start = ((bf16[8,128,512]{1,2,0:T(8,128)(2,1)}), bf16[8,128,512]{1,2,0:T(8,128)(2,1)}, u32[]{:S(2)}, u32[]{:S(2)}) async-start(bf16[8,128,512]{1,2,0:T(8,128)(2,1)} %fusion.85), calls=%async_computation | async-start | bytes 2097152 | tf_op jit(solution)/shard_map/all_to_all | solution.py:90
  22.2 0.7 all-gather.2.cloned.1.call-update
  23.1 0.9 constant_dynamic-slice_fusion.2
  24.0 0.9 fusion.121
  24.9 27.6 %all-to-all-done = bf16[8,128,512]{1,2,0:T(8,128)(2,1)} async-done(((bf16[8,128,512]{1,2,0:T(8,128)(2,1)}), bf16[8,128,512]{1,2,0:T(8,128)(2,1)}, u32[]{:S(2)}, u32[]{:S(2)}) %all-to-all-start) | async-done | bytes 1048608 | tf_op jit(solution)/shard_map/all_to_all | solution.py:90
  52.5 1.5 copy.45
  54.1 1.5 multiply_convert_fusion.7
  55.6 2.0 %copy.46 = bf16[1024,256]{0,1:T(8,128)(2,1)} copy(bf16[1024,256]{1,0:T(8,128)(2,1)} %multiply_convert_fusion.7) | data formatting | bytes 1048576 | tf_op jit(solution)/shard_map/convert_element_type | solution.py:24
  57.6 2.3 %reshape_reshape.3 = bf16[4,256,4,64]{1,0,3,2:T(4,128)(2,1)} reshape(bf16[1024,256]{0,1:T(8,128)(2,1)} %copy.46) | data formatting | bytes 1048576 | tf_op jit(solution)/shard_map/reshape;reshape | solution.py:30
  59.9 12.8 %all-gather.2.cloned.1.call-done = bf16[1024,544]{0,1:T(8,128)(2,1)} async-done(((bf16[128,544]{0,1:T(8,128)(2,1)}), bf16[1024,544]{0,1:T(8,128)(2,1)}) %all-gather.2.cloned.1.call-update) | async-done | bytes 1114128 | tf_op jit(solution)/shard_map/all_gather | solution.py:83
  72.7 0.8 slice.195
  74.1 1.5 slice_convert_fusion
  75.6 2.5 %multiply_convert_fusion.2 = bf16[1024,512]{0,1:T(8,128)(2,1)S(1)} fusion(f32[1024,512]{0,1:T(8,128)S(1)} %slice_convert_fusion, f32[512]{0:T(512)S(1)} %bitcast.243, f32[512]{0:T(512)S(1)} %bitcast.241, f32[512]{0:T(512)S(1)} %bitcast.242, f32[512]{0:T(512)S(1)} %bitcast.240, f32[512]{0:T(512)S(1)} %bitcast.239), kind=kLoop, calls=%fused_computation.17 | loop fusion | flops 6815744 | bytes 3155968 | tf_op jit(solution)/shard_map/convert_element_type | solution.py:24
  78.1 1.2 reshape.114
  79.3 1.2 reshape.113
  80.9 0.7 copy-done.8
  82.1 1.4 fusion.14
  84.0 1.8 copy.66
  85.8 2.7 %reshape.124 = f32[1024,256]{1,0:T(8,128)S(1)} reshape(f32[4,256,4,64]{3,2,1,0:T(4,128)} %copy.66) | data formatting | bytes 2097152 | tf_op jit(solution)/shard_map/convert_element_type | solution.py:110
  88.5 1.5 multiply_reduce_fusion
  90.0 1.4 collective-permute-start
  91.3 2.3 %collective-permute-done = f32[8,128]{1,0:T(8,128)S(1)} collective-permute-done((f32[8,128]{1,0:T(8,128)S(1)}, f32[8,128]{1,0:T(8,128)S(1)}, u32[]{:S(2)}, u32[]{:S(2)}) %collective-permute-start) | collective-permute-done | bytes 4128 | tf_op jit(solution)/shard_map/ppermute | solution.py:62
  93.6 0.7 collective-permute-start.1
  94.4 0.7 constant_dynamic-slice_fusion.9
  95.0 2.2 %collective-permute-done.1 = f32[8,128]{1,0:T(8,128)S(1)} collective-permute-done((f32[8,128]{1,0:T(8,128)S(1)}, f32[8,128]{1,0:T(8,128)S(1)}, u32[]{:S(2)}, u32[]{:S(2)}) %collective-permute-start.1) | collective-permute-done | bytes 4128 | tf_op jit(solution)/shard_map/ppermute | solution.py:62
  97.2 1.3 collective-permute-start.2
  98.6 3.2 %collective-permute-done.2 = f32[8,128]{1,0:T(8,128)S(1)} collective-permute-done((f32[8,128]{1,0:T(8,128)S(1)}, f32[8,128]{1,0:T(8,128)S(1)}, u32[]{:S(2)}, u32[]{:S(2)}) %collective-permute-start.2) | collective-permute-done | bytes 4128 | tf_op jit(solution)/shard_map/ppermute | solution.py:62
  101.8 1.4 multiply_convert_fusion.5
  109.6 1.3 copy-done.6
  111.8 1.0 copy-done.1
  112.8 1.7 copy-done.3
  114.5 1.0 fusion.31
  115.5 1.5 collective-permute-start.6
  116.9 1.3 collective-permute-start.7
  118.6 13.4 %collective-permute-done.8 = bf16[2,2,2,128,256]{4,3,2,0,1:T(8,128)(2,1)} collective-permute-done((bf16[2,2,2,128,256]{4,3,2,0,1:T(8,128)(2,1)S(1)}, bf16[2,2,2,128,256]{4,3,2,0,1:T(8,128)(2,1)}, u32[]{:S(2)}, u32[]{:S(2)}) %collective-permute-start.8) | collective-permute-done | bytes 524320 | tf_op jit(solution)/shard_map/ppermute | solution.py:62
  132.0 3.4 %collective-permute-done.6 = bf16[2,2,2,128,384]{4,3,0,1,2:T(8,128)(2,1)} collective-permute-done((bf16[2,2,2,128,384]{4,3,0,1,2:T(8,128)(2,1)S(1)}, bf16[2,2,2,128,384]{4,3,0,1,2:T(8,128)(2,1)}, u32[]{:S(2)}, u32[]{:S(2)}) %collective-permute-start.6) | collective-permute-done | bytes 786464 | tf_op jit(solution)/shard_map/ppermute | solution.py:62
  135.5 1.4 collective-permute-done.7
  136.9 1.5 bitcast_add_fusion.2
  138.4 1.4 collective-permute-start.15
  139.8 1.5 bitcast_add_fusion
  141.3 0.7 collective-permute-start.12
  142.0 10.3 %collective-permute-done.15 = bf16[2,2,128,256]{3,2,1,0:T(8,128)(2,1)S(1)} collective-permute-done((bf16[2,2,128,256]{3,2,1,0:T(8,128)(2,1)S(1)}, bf16[2,2,128,256]{3,2,1,0:T(8,128)(2,1)S(1)}, u32[]{:S(2)}, u32[]{:S(2)}) %collective-permute-start.15) | collective-permute-done | bytes 262176 | tf_op jit(solution)/shard_map/ppermute | solution.py:62
  152.4 1.0 collective-permute-start.16
  153.3 1.3 bitcast_add_fusion.1
  154.7 1.2 collective-permute-start.9
  155.9 1.9 collective-permute-done.16
  157.8 1.5 collective-permute-start.17
  159.6 6.4 %collective-permute-done.9 = bf16[2,2,128,384]{3,2,0,1:T(8,128)(2,1)S(1)} collective-permute-done((bf16[2,2,128,384]{3,2,0,1:T(8,128)(2,1)S(1)}, bf16[2,2,128,384]{3,2,0,1:T(8,128)(2,1)S(1)}, u32[]{:S(2)}, u32[]{:S(2)}) %collective-permute-start.9) | collective-permute-done | bytes 393248 | tf_op jit(solution)/shard_map/ppermute | solution.py:62
  166.7 1.6 collective-permute-done.13
  168.4 0.6 collective-permute-start.14
  169.0 3.4 %collective-permute-done.10 = bf16[2,128,384]{2,1,0:T(8,128)(2,1)S(1)} collective-permute-done((bf16[2,128,384]{2,1,0:T(8,128)(2,1)S(1)}, bf16[2,128,384]{2,1,0:T(8,128)(2,1)S(1)}, u32[]{:S(2)}, u32[]{:S(2)}) %collective-permute-start.10) | collective-permute-done | bytes 196640 | tf_op jit(solution)/shard_map/ppermute | solution.py:62
  172.5 0.8 collective-permute-start.11
  173.4 5.9 %collective-permute-done.11 = bf16[128,384]{1,0:T(8,128)(2,1)S(1)} collective-permute-done((bf16[128,384]{1,0:T(8,128)(2,1)S(1)}, bf16[128,384]{1,0:T(8,128)(2,1)S(1)}, u32[]{:S(2)}, u32[]{:S(2)}) %collective-permute-start.11) | collective-permute-done | bytes 98336 | tf_op jit(solution)/shard_map/ppermute | solution.py:62
  179.2 0.7 pad_maximum_fusion.3
  (96 shorter events, 11.2 us)
Async XLA Ops:
  6.5 96.6 %copy-start = (bf16[1,256,4096]{2,1,0:T(8,128)(2,1)S(1)}, bf16[1,256,4096]{2,1,0:T(8,128)(2,1)}, u32[]{:S(2)}) copy-start(bf16[1,256,4096]{2,1,0:T(8,128)(2,1)} %param.13) | copy-start | bytes 6291460
  10.3 12.7 %copy-start.10 = (f32[1,2560]{1,0:T(1,128)S(1)}, f32[1,2560]{1,0:T(1,128)}, u32[]{:S(2)}) copy-start(f32[1,2560]{1,0:T(1,128)} %param.9) | copy-start | bytes 30724
  10.3 12.7 %copy-start.11 = (f32[1,32]{1,0:T(1,128)S(1)}, f32[1,32]{1,0:T(1,128)}, u32[]{:S(2)}) copy-start(f32[1,32]{1,0:T(1,128)} %param.10) | copy-start | bytes 388
  10.3 12.7 %copy-start.12 = (f32[1,32]{1,0:T(1,128)S(1)}, f32[1,32]{1,0:T(1,128)}, u32[]{:S(2)}) copy-start(f32[1,32]{1,0:T(1,128)} %param.11) | copy-start | bytes 388
  14.9 37.6 %all-to-all-start = ((bf16[8,128,512]{1,2,0:T(8,128)(2,1)}), bf16[8,128,512]{1,2,0:T(8,128)(2,1)}, u32[]{:S(2)}, u32[]{:S(2)}) async-start(bf16[8,128,512]{1,2,0:T(8,128)(2,1)} %fusion.85), calls=%async_computation | async-start | bytes 2097152 | tf_op jit(solution)/shard_map/all_to_all | solution.py:90
  22.2 50.5 %all-gather.2.cloned.1.call-start = ((), (), s32[]{:S(2)}) async-start(), calls=%async_computation.1 | async-start | bytes 1253376 | tf_op jit(solution)/shard_map/all_gather | solution.py:83
  54.0 3.6 %copy-start.5 = (bf16[8,128,512]{2,1,0:T(8,128)(2,1)}, bf16[8,128,512]{2,1,0:T(8,128)(2,1)S(1)}, u32[]{:S(2)}) copy-start(bf16[8,128,512]{2,1,0:T(8,128)(2,1)S(1)} %copy.45) | copy-start | bytes 3145732
  57.6 18.0 %slice-start = ((f32[1,2560]{1,0:T(1,128)}), f32[1,512]{1,0:T(1,128)S(1)}, s32[]{:S(2)}) async-start(f32[1,2560]{1,0:T(1,128)} %param.9), calls=%async_computation.2 | async-start | bytes 4096 | tf_op jit(solution)/shard_map/slice | solution.py:100
  80.5 1.0 copy-start.8
  80.5 1.3 copy-start.9
  82.1 1.6 copy-start.7
  90.0 3.7 %collective-permute-start = (f32[8,128]{1,0:T(8,128)S(1)}, f32[8,128]{1,0:T(8,128)S(1)}, u32[]{:S(2)}, u32[]{:S(2)}) collective-permute-start(f32[8,128]{1,0:T(8,128)S(1)} %bitcast.238), channel_id=1, source_target_pairs={{0,4},{4,0},{8,12},{12,8},{16,20},{20,16},{24,28},{28,24},{1,5},{5... | collective-permute-start | bytes 12296 | tf_op jit(solution)/shard_map/ppermute | solution.py:62
  93.6 3.6 %collective-permute-start.1 = (f32[8,128]{1,0:T(8,128)S(1)}, f32[8,128]{1,0:T(8,128)S(1)}, u32[]{:S(2)}, u32[]{:S(2)}) collective-permute-start(f32[8,128]{1,0:T(8,128)S(1)} %bitcast_add_fusion.12), channel_id=1, source_target_pairs={{0,8},{4,12},{8,0},{12,4},{16,24},{20,28},{24,16},{28,20},{1,9},{5... | collective-permute-start | bytes 12296 | tf_op jit(solution)/shard_map/ppermute | solution.py:62
  97.2 4.5 %collective-permute-start.2 = (f32[8,128]{1,0:T(8,128)S(1)}, f32[8,128]{1,0:T(8,128)S(1)}, u32[]{:S(2)}, u32[]{:S(2)}) collective-permute-start(f32[8,128]{1,0:T(8,128)S(1)} %fusion.134), channel_id=1, source_target_pairs={{0,16},{4,20},{8,24},{12,28},{16,0},{20,4},{24,8},{28,12},{1,17},{... | collective-permute-start | bytes 12296 | tf_op jit(solution)/shard_map/ppermute | solution.py:62
  104.3 6.6 %collective-permute-start.3 = (bf16[2,1024,384]{2,1,0:T(8,128)(2,1)S(1)}, bf16[2,1024,384]{2,1,0:T(8,128)(2,1)S(1)}, u32[]{:S(2)}, u32[]{:S(2)}) collective-permute-start(bf16[2,1024,384]{2,1,0:T(8,128)(2,1)S(1)} %pad_maximum_fusion), channel_id=1, source_target_pairs={{0,1},{1,0},{2,3},{3,2},{4,5},{5,4},{6,7},{7,6},{8,9},{9,8},{10,11... | collective-permute-start | bytes 4718600 | tf_op jit(solution)/shard_map/ppermute | solution.py:62
  105.5 3.7 %collective-permute-start.5 = (bf16[2,1024,256]{2,1,0:T(8,128)(2,1)S(1)}, bf16[2,1024,256]{2,1,0:T(8,128)(2,1)S(1)}, u32[]{:S(2)}, u32[]{:S(2)}) collective-permute-start(bf16[2,1024,256]{2,1,0:T(8,128)(2,1)S(1)} %pad_maximum_fusion.2), channel_id=1, source_target_pairs={{0,1},{1,0},{2,3},{3,2},{4,5},{5,4},{6,7},{7,6},{8,9},{9,8},{10,11... | collective-permute-start | bytes 3145736 | tf_op jit(solution)/shard_map/ppermute | solution.py:62
  106.7 4.8 %collective-permute-start.4 = (bf16[2,1024,384]{2,1,0:T(8,128)(2,1)S(1)}, bf16[2,1024,384]{2,1,0:T(8,128)(2,1)S(1)}, u32[]{:S(2)}, u32[]{:S(2)}) collective-permute-start(bf16[2,1024,384]{2,1,0:T(8,128)(2,1)S(1)} %pad_maximum_fusion.1), channel_id=1, source_target_pairs={{0,1},{1,0},{2,3},{3,2},{4,5},{5,4},{6,7},{7,6},{8,9},{9,8},{10,11... | collective-permute-start | bytes 4718600 | tf_op jit(solution)/shard_map/ppermute | solution.py:62
  109.5 1.4 copy-start.6
  111.2 1.6 copy-start.1
  112.8 1.7 copy-start.3
  115.5 20.0 %collective-permute-start.6 = (bf16[2,2,2,128,384]{4,3,0,1,2:T(8,128)(2,1)S(1)}, bf16[2,2,2,128,384]{4,3,0,1,2:T(8,128)(2,1)}, u32[]{:S(2)}, u32[]{:S(2)}) collective-permute-start(bf16[2,2,2,128,384]{4,3,0,1,2:T(8,128)(2,1)S(1)} %fusion.30), channel_id=1, source_target_pairs={{0,2},{1,3},{2,0},{3,1},{4,6},{5,7},{6,4},{7,5},{8,10},{9,11},{10,... | collective-permute-start | bytes 2359304 | tf_op jit(solution)/shard_map/ppermute | solution.py:62
  116.9 19.9 %collective-permute-start.7 = (bf16[2,2,2,128,384]{4,3,0,1,2:T(8,128)(2,1)}, bf16[2,2,2,128,384]{4,3,0,1,2:T(8,128)(2,1)}, u32[]{:S(2)}, u32[]{:S(2)}) collective-permute-start(bf16[2,2,2,128,384]{4,3,0,1,2:T(8,128)(2,1)} %fusion.31), channel_id=1, source_target_pairs={{0,4},{4,0},{8,12},{12,8},{16,20},{20,16},{24,28},{28,24},{1,5},{5... | collective-permute-start | bytes 2359304 | tf_op jit(solution)/shard_map/ppermute | solution.py:62
  118.2 13.8 %collective-permute-start.8 = (bf16[2,2,2,128,256]{4,3,2,0,1:T(8,128)(2,1)S(1)}, bf16[2,2,2,128,256]{4,3,2,0,1:T(8,128)(2,1)}, u32[]{:S(2)}, u32[]{:S(2)}) collective-permute-start(bf16[2,2,2,128,256]{4,3,2,0,1:T(8,128)(2,1)S(1)} %fusion.32), channel_id=1, source_target_pairs={{0,8},{4,12},{8,0},{12,4},{16,24},{20,28},{24,16},{28,20},{1,9},{5... | collective-permute-start | bytes 1572872 | tf_op jit(solution)/shard_map/ppermute | solution.py:62
  118.6 21.2 %copy-start.4 = (f32[2,1024,384]{2,1,0:T(8,128)S(1)}, f32[2,1024,384]{2,1,0:T(8,128)}, u32[]{:S(2)}) copy-start(f32[2,1024,384]{2,1,0:T(8,128)} %copy-done.3) | copy-start | bytes 9437188
  138.4 13.9 %collective-permute-start.15 = (bf16[2,2,128,256]{3,2,1,0:T(8,128)(2,1)S(1)}, bf16[2,2,128,256]{3,2,1,0:T(8,128)(2,1)S(1)}, u32[]{:S(2)}, u32[]{:S(2)}) collective-permute-start(bf16[2,2,128,256]{3,2,1,0:T(8,128)(2,1)S(1)} %fusion.51), channel_id=1, source_target_pairs={{0,16},{4,20},{8,24},{12,28},{16,0},{20,4},{24,8},{28,12},{1,17},{... | collective-permute-start | bytes 786440 | tf_op jit(solution)/shard_map/ppermute | solution.py:62
  139.8 13.6 %copy-start.2 = (f32[2,1024,384]{2,1,0:T(8,128)S(1)}, f32[2,1024,384]{2,1,0:T(8,128)}, u32[]{:S(2)}) copy-start(f32[2,1024,384]{2,1,0:T(8,128)} %copy-done.1) | copy-start | bytes 9437188
  141.3 18.1 %collective-permute-start.12 = (bf16[2,2,128,384]{3,2,0,1:T(8,128)(2,1)S(1)}, bf16[2,2,128,384]{3,2,0,1:T(8,128)(2,1)S(1)}, u32[]{:S(2)}, u32[]{:S(2)}) collective-permute-start(bf16[2,2,128,384]{3,2,0,1:T(8,128)(2,1)S(1)} %fusion.50), channel_id=1, source_target_pairs={{0,8},{4,12},{8,0},{12,4},{16,24},{20,28},{24,16},{28,20},{1,9},{5... | collective-permute-start | bytes 1179656 | tf_op jit(solution)/shard_map/ppermute | solution.py:62
  152.4 5.4 %collective-permute-start.16 = (bf16[2,128,256]{2,1,0:T(8,128)(2,1)S(1)}, bf16[2,128,256]{2,1,0:T(8,128)(2,1)S(1)}, u32[]{:S(2)}, u32[]{:S(2)}) collective-permute-start(bf16[2,128,256]{2,1,0:T(8,128)(2,1)S(1)} %fusion.77), channel_id=1, source_target_pairs={{0,2},{1,3},{2,0},{3,1},{4,6},{5,7},{6,4},{7,5},{8,10},{9,11},{10,... | collective-permute-start | bytes 393224 | tf_op jit(solution)/shard_map/ppermute | solution.py:62
  154.7 11.3 %collective-permute-start.9 = (bf16[2,2,128,384]{3,2,0,1:T(8,128)(2,1)S(1)}, bf16[2,2,128,384]{3,2,0,1:T(8,128)(2,1)S(1)}, u32[]{:S(2)}, u32[]{:S(2)}) collective-permute-start(bf16[2,2,128,384]{3,2,0,1:T(8,128)(2,1)S(1)} %fusion.49), channel_id=1, source_target_pairs={{0,4},{4,0},{8,12},{12,8},{16,20},{20,16},{24,28},{28,24},{1,5},{5... | collective-permute-start | bytes 1179656 | tf_op jit(solution)/shard_map/ppermute | solution.py:62
  157.8 8.9 %collective-permute-start.17 = (bf16[128,256]{1,0:T(8,128)(2,1)S(1)}, bf16[128,256]{1,0:T(8,128)(2,1)S(1)}, u32[]{:S(2)}, u32[]{:S(2)}) collective-permute-start(bf16[128,256]{1,0:T(8,128)(2,1)S(1)} %fusion.97), channel_id=1, source_target_pairs={{0,4},{4,0},{8,12},{12,8},{16,20},{20,16},{24,28},{28,24},{1,5},{5... | collective-permute-start | bytes 196616 | tf_op jit(solution)/shard_map/ppermute | solution.py:62
  159.5 8.9 %collective-permute-start.13 = (bf16[2,128,384]{2,1,0:T(8,128)(2,1)S(1)}, bf16[2,128,384]{2,1,0:T(8,128)(2,1)S(1)}, u32[]{:S(2)}, u32[]{:S(2)}) collective-permute-start(bf16[2,128,384]{2,1,0:T(8,128)(2,1)S(1)} %fusion.58), channel_id=1, source_target_pairs={{0,16},{4,20},{8,24},{12,28},{16,0},{20,4},{24,8},{28,12},{1,17},{... | collective-permute-start | bytes 589832 | tf_op jit(solution)/shard_map/ppermute | solution.py:62
  166.2 6.3 %collective-permute-start.10 = (bf16[2,128,384]{2,1,0:T(8,128)(2,1)S(1)}, bf16[2,128,384]{2,1,0:T(8,128)(2,1)S(1)}, u32[]{:S(2)}, u32[]{:S(2)}) collective-permute-start(bf16[2,128,384]{2,1,0:T(8,128)(2,1)S(1)} %fusion.57), channel_id=1, source_target_pairs={{0,8},{4,12},{8,0},{12,4},{16,24},{20,28},{24,16},{28,20},{1,9},{5... | collective-permute-start | bytes 589832 | tf_op jit(solution)/shard_map/ppermute | solution.py:62
  168.4 4.9 %collective-permute-start.14 = (bf16[128,384]{1,0:T(8,128)(2,1)S(1)}, bf16[128,384]{1,0:T(8,128)(2,1)S(1)}, u32[]{:S(2)}, u32[]{:S(2)}) collective-permute-start(bf16[128,384]{1,0:T(8,128)(2,1)S(1)} %fusion.96), channel_id=1, source_target_pairs={{0,2},{1,3},{2,0},{3,1},{4,6},{5,7},{6,4},{7,5},{8,10},{9,11},{10,... | collective-permute-start | bytes 294920 | tf_op jit(solution)/shard_map/ppermute | solution.py:62
  172.5 6.7 %collective-permute-start.11 = (bf16[128,384]{1,0:T(8,128)(2,1)S(1)}, bf16[128,384]{1,0:T(8,128)(2,1)S(1)}, u32[]{:S(2)}, u32[]{:S(2)}) collective-permute-start(bf16[128,384]{1,0:T(8,128)(2,1)S(1)} %fusion.95), channel_id=1, source_target_pairs={{0,16},{4,20},{8,24},{12,28},{16,0},{20,4},{24,8},{28,12},{1,17},{... | collective-permute-start | bytes 294920 | tf_op jit(solution)/shard_map/ppermute | solution.py:62
Sparse Core Ops, SparseCore 0:
  25.1 47.5 all-gather.1

commit v4 on v3

--- a/solution.py
+++ b/solution.py
@@ -70,6 +70,19 @@
     return [1 << i for i in range(size.bit_length() - 1)]
 
 
+def gather_tokens(rows, order):
+    whole = rows
+    held = []
+    for bit in order:
+        other = exchange(whole, "ctx", bit)
+        place = sum(1 for done in held if done > bit)
+        own_first = jnp.stack([whole, other], axis=place)
+        own_last = jnp.stack([other, whole], axis=place)
+        whole = jnp.where(my_bit("ctx", bit) == 0, own_first, own_last)
+        held.append(bit)
+    return whole
+
+
 def on_device(projected, conv_weight, conv_bias, step_bias, log_rates, norm_gain, out_weight):
     rows = projected.shape[0]
     devices = lax.axis_size("ctx")
@@ -80,7 +93,8 @@
     here = projected[:, 0]
 
     tail_columns, here = lax.optimization_barrier((here[:, 2 * GCH :], here))
-    shared = lax.all_gather(tail_columns, "ctx", axis=0, tiled=True)
+    shared = gather_tokens(tail_columns, bits_of(devices)[::-1])
+    shared = shared.reshape(devices * rows, tail_columns.shape[1])
     parts = [
         jnp.concatenate(
             [here[:, d * width : (d + 1) * width], here[:, GCH + d * width : GCH + (d + 1) * width]], axis=1

time: 188 us -> 193 us (1.027)
  waiting for transfers between devices: 97.3 us -> 76.6 us
  between operations: 13.9 us -> 0.53 us
  starting transfers between devices: 21.9 us -> 34.7 us
  other arithmetic: 20.9 us -> 33.5 us
  local copies, waits for them, and re-layouts: 25.4 us -> 36 us
  matrix products: 7.42 us -> 10.6 us
    all_to_all x1, waiting for transfers between devices: 27.6 us -> 0.01 us  [on_device(): lax.all_to_all(jnp.stack(parts), 'ctx', split_axis=0, concat_axis=0, tile...]
    ppermute x18 -> x21, waiting for transfers between devices: 56.2 us -> 76.6 us  [exchange(): return lax.ppermute(array, axis, [(i, i ^ bit) for i in range(peers)])]
    ppermute x18 -> x21, starting transfers between devices: 14.6 us -> 30.9 us  [exchange(): return lax.ppermute(array, axis, [(i, i ^ bit) for i in range(peers)])]
    all_gather x1 -> x0, waiting for transfers between devices: 12.8 us -> none  [on_device(): shared = lax.all_gather(tail_columns, 'ctx', axis=0, tiled=True)]
    select_n x0 -> x5, other arithmetic: none -> 10.4 us  [gather_tokens(): whole = jnp.where(my_bit('ctx', bit) == 0, own_first, own_last)]
    select_n x0 -> x3, local copies, waits for them, and re-layouts: none -> 9.76 us  [gather_tokens(): whole = jnp.where(my_bit('ctx', bit) == 0, own_first, own_last)]
    all_to_all x1, starting transfers between devices: 7.28 us -> 3.81 us  [on_device(): lax.all_to_all(jnp.stack(parts), 'ctx', split_axis=0, concat_axis=0, tile...]
    slice x0 -> x2, local copies, waits for them, and re-layouts: none -> 3.08 us  [on_device(): keys[:, :N]]
  transfers between devices with their start and end apart: 20 -> 22, of which waited for: 17 -> 17; matrix products, arithmetic and copies ran while one was open for 10% -> 27% of each run, Pallas kernels for 0% -> 0%
where the time goes in v4:
time: 193 us; the launch traced here: 192 us
  waiting for transfers between devices  76.6 us (40%)
  local copies, waits for them, and re-layouts  36 us (19%)
  starting transfers between devices  34.7 us (18%)
  other arithmetic  33.5 us (17%)
  matrix products  10.6 us (5%)
    ppermute x21, waiting for transfers between devices, exchange(): return lax.ppermute(array, axis, [(i, i ^ bit) for i in range(peers)])  76.6 us
    ppermute x21, starting transfers between devices, exchange(): return lax.ppermute(array, axis, [(i, i ^ bit) for i in range(peers)])  30.9 us
    select_n x5, other arithmetic, gather_tokens(): whole = jnp.where(my_bit('ctx', bit) == 0, own_first, own_last)  10.4 us
    select_n x3, local copies, waits for them, and re-layouts, gather_tokens(): whole = jnp.where(my_bit('ctx', bit) == 0, own_first, own_last)  9.76 us
    unnamed x27, local copies, waits for them, and re-layouts  5.98 us
    dot_general x12, matrix products, product(): pieces.append(jnp.dot(normed, block, preferred_element_type=F32))  4.73 us
    unnamed x7, other arithmetic  4.62 us
    convert_element_type x2, local copies, waits for them, and re-layouts, on_device(): gated = scanned.astype(F32) * jax.nn.silu(moved[:, :width].astype(F32))  4.46 us
  transfers between devices with their start and end apart: 22, of which 17 were waited for; matrix products, arithmetic and copies ran while one was open for 27% of the time, Pallas kernels for 0%

profile of v4, /device:TPU:0, one launch (start us, length us, event | category | flops | bytes accessed | tf_op | source)
XLA Modules:
  0.0 191.9 jit_solution(10565621277141025531)
XLA Ops:
  0.0 1.9 copy.30
  1.9 4.1 %collective-permute-start = (bf16[128,544]{1,0:T(8,128)(2,1)S(1)}, bf16[128,544]{1,0:T(8,128)(2,1)}, u32[]{:S(2)}, u32[]{:S(2)}) collective-permute-start(bf16[128,544]{1,0:T(8,128)(2,1)S(1)} %slice.194), channel_id=1, source_target_pairs={{0,16},{4,20},{8,24},{12,28},{16,0},{20,4},{24,8},{28,12},{1,17},{... | collective-permute-start | bytes 417800 | tf_op jit(solution)/shard_map/ppermute | solution.py:62
  11.4 3.8 %all-to-all-start = ((bf16[8,128,512]{2,1,0:T(8,128)(2,1)}), bf16[8,128,512]{2,1,0:T(8,128)(2,1)S(1)}, u32[]{:S(2)}, u32[]{:S(2)}) async-start(bf16[8,128,512]{2,1,0:T(8,128)(2,1)} %fusion.78), calls=%async_computation | async-start | bytes 2097152 | tf_op jit(solution)/shard_map/all_to_all | solution.py:104
  15.3 0.9 constant_dynamic-slice_fusion.2
  16.2 1.8 maximum_select_fusion.4
  18.0 2.0 %collective-permute-start.1 = (bf16[2,128,544]{2,1,0:T(8,128)(2,1)}, bf16[2,128,544]{2,1,0:T(8,128)(2,1)}, u32[]{:S(2)}, u32[]{:S(2)}) collective-permute-start(bf16[2,128,544]{2,1,0:T(8,128)(2,1)} %maximum_select_fusion.4), channel_id=1, source_target_pairs={{0,8},{4,12},{8,0},{12,4},{16,24},{20,28},{24,16},{28,20},{1,9},{5... | collective-permute-start | bytes 835592 | tf_op jit(solution)/shard_map/ppermute | solution.py:62
  20.0 1.1 maximum_select_fusion.3
  21.1 20.2 %collective-permute-done.1 = bf16[2,128,544]{2,1,0:T(8,128)(2,1)} collective-permute-done((bf16[2,128,544]{2,1,0:T(8,128)(2,1)}, bf16[2,128,544]{2,1,0:T(8,128)(2,1)}, u32[]{:S(2)}, u32[]{:S(2)}) %collective-permute-start.1) | collective-permute-done | bytes 278560 | tf_op jit(solution)/shard_map/ppermute | solution.py:62
  41.3 2.2 %maximum_select_fusion.2 = bf16[2,2,128,544]{3,2,0,1:T(8,128)(2,1)} fusion(bf16[2,1,128,544]{3,2,0,1:T(8,128)(2,1)} %bitcast.7, bf16[2,1,128,544]{3,2,0,1:T(8,128)(2,1)S(1)} %maximum_select_fusion.3, pred[]{:T(512)S(6)} %eq.27), kind=kLoop, calls=%fused_computation.76 | loop fusion | flops 835584 | bytes 1114113 | tf_op jit(solution)/shard_map/jit(_where)/select_n | solution.py:81
  43.5 2.2 %copy.31 = bf16[2,2,128,544]{2,3,1,0:T(8,128)(2,1)} copy(bf16[2,2,128,544]{3,2,0,1:T(8,128)(2,1)} %maximum_select_fusion.2) | data formatting | bytes 1114112 | tf_op jit(solution)/shard_map/jit(_where)/select_n | solution.py:81
  45.6 1.4 collective-permute-start.2
  48.0 1.1 fusion.133
  49.1 2.2 %maximum_select_fusion.1 = bf16[2,2,1,128,544]{4,3,0,2,1:T(8,128)(2,1)} fusion(bf16[2,1,1,128,544]{4,3,0,2,1:T(8,128)(2,1)} %bitcast.6, bf16[2,1,1,128,544]{4,3,0,2,1:T(8,128)(2,1)S(1)} %fusion.133, pred[]{:T(512)S(6)} %eq.27), kind=kLoop, calls=%fused_computation.75 | loop fusion | flops 835584 | bytes 1114113 | tf_op jit(solution)/shard_map/jit(_where)/select_n | solution.py:81
  51.3 5.7 %collective-permute-done.2 = bf16[2,2,128,544]{2,3,1,0:T(8,128)(2,1)} collective-permute-done((bf16[2,2,128,544]{2,3,1,0:T(8,128)(2,1)}, bf16[2,2,128,544]{2,3,1,0:T(8,128)(2,1)}, u32[]{:S(2)}, u32[]{:S(2)}) %collective-permute-start.2) | collective-permute-done | bytes 557088 | tf_op jit(solution)/shard_map/ppermute | solution.py:62
  56.9 2.1 %copy.32 = bf16[2,2,128,544]{3,2,0,1:T(8,128)(2,1)} copy(bf16[2,2,128,544]{2,3,1,0:T(8,128)(2,1)} %collective-permute-done.2) | data formatting | bytes 1114112 | tf_op jit(solution)/shard_map/ppermute | solution.py:62
  59.1 3.1 %maximum_select_fusion = bf16[2,2,2,128,544]{4,3,0,2,1:T(8,128)(2,1)} fusion(bf16[2,2,1,128,544]{4,3,0,2,1:T(8,128)(2,1)} %bitcast.245, bf16[2,2,1,128,544]{4,3,0,2,1:T(8,128)(2,1)} %maximum_select_fusion.1, pred[]{:T(512)S(6)} %eq.26), kind=kLoop, calls=%fused_computation.43 | loop fusion | flops 1671168 | bytes 2228225 | tf_op jit(solution)/shard_map/jit(_where)/select_n | solution.py:81
  62.2 3.9 %copy.33 = bf16[2,2,2,128,544]{3,2,1,0,4:T(2,128)(2,1)} copy(bf16[2,2,2,128,544]{4,3,0,2,1:T(8,128)(2,1)} %maximum_select_fusion) | data formatting | bytes 2228224 | tf_op jit(solution)/shard_map/jit(_where)/select_n | solution.py:81
  66.1 3.7 %select_n.253 = bf16[1024,544]{0,1:T(8,128)(2,1)} reshape(bf16[2,2,2,128,544]{3,2,1,0,4:T(2,128)(2,1)} %copy.33) | data formatting | bytes 2228224 | tf_op jit(solution)/shard_map/jit(_where)/select_n | solution.py:81
  69.8 1.5 slice_convert_fusion
  71.3 2.5 %multiply_convert_fusion.2 = bf16[1024,512]{0,1:T(8,128)(2,1)S(1)} fusion(f32[1024,512]{0,1:T(8,128)S(1)} %slice_convert_fusion, f32[512]{0:T(512)S(1)} %bitcast.258, f32[512]{0:T(512)S(1)} %bitcast.256, f32[512]{0:T(512)S(1)} %bitcast.257, f32[512]{0:T(512)S(1)} %bitcast.255, f32[512]{0:T(512)S(1)} %bitcast.254), kind=kLoop, calls=%fused_computation.17 | loop fusion | flops 6815744 | bytes 3155968 | tf_op jit(solution)/shard_map/convert_element_type | solution.py:24
  73.8 1.0 fusion.113
  74.8 2.0 %copy.34 = bf16[1024,256]{1,0:T(8,128)(2,1)} copy(bf16[1024,256]{0,1:T(8,128)(2,1)} %get-tuple-element.41) | data formatting | bytes 1048576 | tf_op jit(solution)/shard_map/slice | solution.py:121
  76.8 2.0 %copy.35 = bf16[1024,256]{1,0:T(8,128)(2,1)} copy(bf16[1024,256]{0,1:T(8,128)(2,1)} %get-tuple-element.40) | data formatting | bytes 1048576 | tf_op jit(solution)/shard_map/slice | solution.py:121
  79.5 2.5 %fusion.115 = f32[4,256,256]{2,1,0:T(8,128)} fusion(bf16[4,256,256]{2,1,0:T(8,128)(2,1)} %bitcast.241, bf16[4,256,256]{2,1,0:T(8,128)(2,1)} %bitcast.243), kind=kOutput, calls=%fused_computation.214 | convolution fusion | flops 134217728 | bytes 2097152 | tf_op jit(solution)/shard_map/btn,bsn->bts/dot_general | solution.py:38
  82.2 1.5 multiply_convert_fusion.7
  83.7 2.1 %copy.36 = bf16[1024,256]{0,1:T(8,128)(2,1)} copy(bf16[1024,256]{1,0:T(8,128)(2,1)} %multiply_convert_fusion.7) | data formatting | bytes 1048576 | tf_op jit(solution)/shard_map/convert_element_type | solution.py:24
  85.7 2.3 %reshape_reshape.3 = bf16[4,256,4,64]{1,0,3,2:T(4,128)(2,1)} reshape(bf16[1024,256]{0,1:T(8,128)(2,1)} %copy.36) | data formatting | bytes 1048576 | tf_op jit(solution)/shard_map/reshape;reshape | solution.py:30
  88.0 1.4 multiply_convert_fusion.6
  89.4 1.3 fusion.39
  90.7 1.4 fusion.14
  92.6 1.8 copy.50
  94.4 2.7 %reshape.305 = f32[1024,256]{1,0:T(8,128)S(1)} reshape(f32[4,256,4,64]{3,2,1,0:T(4,128)} %copy.50) | data formatting | bytes 2097152 | tf_op jit(solution)/shard_map/convert_element_type | solution.py:124
  97.1 1.5 multiply_reduce_fusion
  98.6 1.8 collective-permute-start.3
  100.4 1.9 collective-permute-done.3
  102.2 2.5 %collective-permute-start.4 = (f32[8,128]{1,0:T(8,128)S(1)}, f32[8,128]{1,0:T(8,128)S(1)}, u32[]{:S(2)}, u32[]{:S(2)}) collective-permute-start(f32[8,128]{1,0:T(8,128)S(1)} %bitcast_add_fusion.12), channel_id=1, source_target_pairs={{0,8},{4,12},{8,0},{12,4},{16,24},{20,28},{24,16},{28,20},{1,9},{5... | collective-permute-start | bytes 12296 | tf_op jit(solution)/shard_map/ppermute | solution.py:62
  105.4 0.9 collective-permute-done.4
  106.3 4.0 %collective-permute-start.5 = (f32[8,128]{1,0:T(8,128)S(1)}, f32[8,128]{1,0:T(8,128)S(1)}, u32[]{:S(2)}, u32[]{:S(2)}) collective-permute-start(f32[8,128]{1,0:T(8,128)S(1)} %fusion.132), channel_id=1, source_target_pairs={{0,16},{4,20},{8,24},{12,28},{16,0},{20,4},{24,8},{28,12},{1,17},{... | collective-permute-start | bytes 12296 | tf_op jit(solution)/shard_map/ppermute | solution.py:62
  110.3 1.6 collective-permute-done.5
  111.9 1.4 multiply_convert_fusion.5
  119.7 1.3 copy-done.6
  121.9 1.1 copy-done.1
  123.0 1.7 copy-done.3
  124.6 1.0 fusion.31
  125.6 1.5 collective-permute-start.9
  127.1 1.4 collective-permute-start.10
  128.5 1.1 collective-permute-start.11
  129.6 12.7 %collective-permute-done.11 = bf16[2,2,2,128,256]{4,3,2,0,1:T(8,128)(2,1)} collective-permute-done((bf16[2,2,2,128,256]{4,3,2,0,1:T(8,128)(2,1)S(1)}, bf16[2,2,2,128,256]{4,3,2,0,1:T(8,128)(2,1)}, u32[]{:S(2)}, u32[]{:S(2)}) %collective-permute-start.11) | collective-permute-done | bytes 524320 | tf_op jit(solution)/shard_map/ppermute | solution.py:62
  142.3 3.3 %collective-permute-done.9 = bf16[2,2,2,128,384]{4,3,0,1,2:T(8,128)(2,1)} collective-permute-done((bf16[2,2,2,128,384]{4,3,0,1,2:T(8,128)(2,1)S(1)}, bf16[2,2,2,128,384]{4,3,0,1,2:T(8,128)(2,1)}, u32[]{:S(2)}, u32[]{:S(2)}) %collective-permute-start.9) | collective-permute-done | bytes 786464 | tf_op jit(solution)/shard_map/ppermute | solution.py:62
  145.6 1.4 collective-permute-done.10
  147.0 1.5 bitcast_add_fusion.2
  148.6 3.0 %collective-permute-start.18 = (bf16[2,2,128,256]{3,2,1,0:T(8,128)(2,1)S(1)}, bf16[2,2,128,256]{3,2,1,0:T(8,128)(2,1)S(1)}, u32[]{:S(2)}, u32[]{:S(2)}) collective-permute-start(bf16[2,2,128,256]{3,2,1,0:T(8,128)(2,1)S(1)} %fusion.44), channel_id=1, source_target_pairs={{0,16},{4,20},{8,24},{12,28},{16,0},{20,4},{24,8},{28,12},{1,17},{... | collective-permute-start | bytes 786440 | tf_op jit(solution)/shard_map/ppermute | solution.py:62
  151.6 1.5 bitcast_add_fusion
  153.1 1.7 collective-permute-start.15
  154.8 8.3 %collective-permute-done.18 = bf16[2,2,128,256]{3,2,1,0:T(8,128)(2,1)S(1)} collective-permute-done((bf16[2,2,128,256]{3,2,1,0:T(8,128)(2,1)S(1)}, bf16[2,2,128,256]{3,2,1,0:T(8,128)(2,1)S(1)}, u32[]{:S(2)}, u32[]{:S(2)}) %collective-permute-start.18) | collective-permute-done | bytes 262176 | tf_op jit(solution)/shard_map/ppermute | solution.py:62
  163.8 1.3 bitcast_add_fusion.1
  165.2 1.4 collective-permute-start.12
  166.6 1.6 collective-permute-done.19
  168.3 1.6 collective-permute-start.20
  170.0 6.0 %collective-permute-done.12 = bf16[2,2,128,384]{3,2,0,1:T(8,128)(2,1)S(1)} collective-permute-done((bf16[2,2,128,384]{3,2,0,1:T(8,128)(2,1)S(1)}, bf16[2,2,128,384]{3,2,0,1:T(8,128)(2,1)S(1)}, u32[]{:S(2)}, u32[]{:S(2)}) %collective-permute-start.12) | collective-permute-done | bytes 393248 | tf_op jit(solution)/shard_map/ppermute | solution.py:62
  176.2 1.4 collective-permute-start.13
  177.6 3.0 %collective-permute-done.16 = bf16[2,128,384]{2,1,0:T(8,128)(2,1)S(1)} collective-permute-done((bf16[2,128,384]{2,1,0:T(8,128)(2,1)S(1)}, bf16[2,128,384]{2,1,0:T(8,128)(2,1)S(1)}, u32[]{:S(2)}, u32[]{:S(2)}) %collective-permute-start.16) | collective-permute-done | bytes 196640 | tf_op jit(solution)/shard_map/ppermute | solution.py:62
  181.3 3.2 %collective-permute-done.13 = bf16[2,128,384]{2,1,0:T(8,128)(2,1)S(1)} collective-permute-done((bf16[2,128,384]{2,1,0:T(8,128)(2,1)S(1)}, bf16[2,128,384]{2,1,0:T(8,128)(2,1)S(1)}, u32[]{:S(2)}, u32[]{:S(2)}) %collective-permute-start.13) | collective-permute-done | bytes 196640 | tf_op jit(solution)/shard_map/ppermute | solution.py:62
  185.4 5.8 %collective-permute-done.14 = bf16[128,384]{1,0:T(8,128)(2,1)S(1)} collective-permute-done((bf16[128,384]{1,0:T(8,128)(2,1)S(1)}, bf16[128,384]{1,0:T(8,128)(2,1)S(1)}, u32[]{:S(2)}, u32[]{:S(2)}) %collective-permute-start.14) | collective-permute-done | bytes 98336 | tf_op jit(solution)/shard_map/ppermute | solution.py:62
  (110 shorter events, 18.8 us)
Async XLA Ops:
  0.0 113.3 %copy-start = (bf16[1,256,4096]{2,1,0:T(8,128)(2,1)S(1)}, bf16[1,256,4096]{2,1,0:T(8,128)(2,1)}, u32[]{:S(2)}) copy-start(bf16[1,256,4096]{2,1,0:T(8,128)(2,1)} %param.13) | copy-start | bytes 6291460
  1.9 14.3 %collective-permute-start = (bf16[128,544]{1,0:T(8,128)(2,1)S(1)}, bf16[128,544]{1,0:T(8,128)(2,1)}, u32[]{:S(2)}, u32[]{:S(2)}) collective-permute-start(bf16[128,544]{1,0:T(8,128)(2,1)S(1)} %slice.194), channel_id=1, source_target_pairs={{0,16},{4,20},{8,24},{12,28},{16,0},{20,4},{24,8},{28,12},{1,17},{... | collective-permute-start | bytes 417800 | tf_op jit(solution)/shard_map/ppermute | solution.py:62
  8.1 11.9 %copy-start.10 = (f32[1,2560]{1,0:T(1,128)S(1)}, f32[1,2560]{1,0:T(1,128)}, u32[]{:S(2)}) copy-start(f32[1,2560]{1,0:T(1,128)} %param.9) | copy-start | bytes 30724
  11.4 70.7 %all-to-all-start = ((bf16[8,128,512]{2,1,0:T(8,128)(2,1)}), bf16[8,128,512]{2,1,0:T(8,128)(2,1)S(1)}, u32[]{:S(2)}, u32[]{:S(2)}) async-start(bf16[8,128,512]{2,1,0:T(8,128)(2,1)} %fusion.78), calls=%async_computation | async-start | bytes 2097152 | tf_op jit(solution)/shard_map/all_to_all | solution.py:104
  15.2 31.9 %copy-start.11 = (f32[1,32]{1,0:T(1,128)S(1)}, f32[1,32]{1,0:T(1,128)}, u32[]{:S(2)}) copy-start(f32[1,32]{1,0:T(1,128)} %param.10) | copy-start | bytes 388
  15.2 31.8 %copy-start.12 = (f32[1,32]{1,0:T(1,128)S(1)}, f32[1,32]{1,0:T(1,128)}, u32[]{:S(2)}) copy-start(f32[1,32]{1,0:T(1,128)} %param.11) | copy-start | bytes 388
  18.0 23.3 %collective-permute-start.1 = (bf16[2,128,544]{2,1,0:T(8,128)(2,1)}, bf16[2,128,544]{2,1,0:T(8,128)(2,1)}, u32[]{:S(2)}, u32[]{:S(2)}) collective-permute-start(bf16[2,128,544]{2,1,0:T(8,128)(2,1)} %maximum_select_fusion.4), channel_id=1, source_target_pairs={{0,8},{4,12},{8,0},{12,4},{16,24},{20,28},{24,16},{28,20},{1,9},{5... | collective-permute-start | bytes 835592 | tf_op jit(solution)/shard_map/ppermute | solution.py:62
  45.6 11.3 %collective-permute-start.2 = (bf16[2,2,128,544]{2,3,1,0:T(8,128)(2,1)}, bf16[2,2,128,544]{2,3,1,0:T(8,128)(2,1)}, u32[]{:S(2)}, u32[]{:S(2)}) collective-permute-start(bf16[2,2,128,544]{2,3,1,0:T(8,128)(2,1)} %copy.31), channel_id=1, source_target_pairs={{0,4},{4,0},{8,12},{12,8},{16,20},{20,16},{24,28},{28,24},{1,5},{5... | collective-permute-start | bytes 1671176 | tf_op jit(solution)/shard_map/ppermute | solution.py:62
  69.8 1.5 slice-start.1
  73.8 5.1 %slice-start = ((bf16[1024,544]{0,1:T(8,128)(2,1)}), bf16[1024,32]{0,1:T(8,128)(2,1)S(1)}, s32[]{:S(2)}) async-start(bf16[1024,544]{0,1:T(8,128)(2,1)} %select_n.253), calls=%async_computation.1 | async-start | bytes 131072 | tf_op jit(solution)/shard_map/slice | solution.py:116
  82.1 3.6 %copy-start.5 = (bf16[8,128,512]{2,1,0:T(8,128)(2,1)}, bf16[8,128,512]{2,1,0:T(8,128)(2,1)S(1)}, u32[]{:S(2)}) copy-start(bf16[8,128,512]{2,1,0:T(8,128)(2,1)S(1)} %all-to-all-done) | copy-start | bytes 3145732
  88.0 2.7 %copy-start.8 = (bf16[4,256,4,64]{1,0,3,2:T(4,128)(2,1)S(1)}, bf16[4,256,4,64]{1,0,3,2:T(4,128)(2,1)}, u32[]{:S(2)}) copy-start(bf16[4,256,4,64]{1,0,3,2:T(4,128)(2,1)} %reshape_reshape.3) | copy-start | bytes 1572868
  88.0 2.7 %copy-start.9 = (f32[4,256,256]{2,1,0:T(8,128)S(1)}, f32[4,256,256]{2,1,0:T(8,128)}, u32[]{:S(2)}) copy-start(f32[4,256,256]{2,1,0:T(8,128)} %fusion.115) | copy-start | bytes 3145732
  90.7 1.6 copy-start.7
  98.6 3.7 %collective-permute-start.3 = (f32[8,128]{1,0:T(8,128)S(1)}, f32[8,128]{1,0:T(8,128)S(1)}, u32[]{:S(2)}, u32[]{:S(2)}) collective-permute-start(f32[8,128]{1,0:T(8,128)S(1)} %bitcast.253), channel_id=1, source_target_pairs={{0,4},{4,0},{8,12},{12,8},{16,20},{20,16},{24,28},{28,24},{1,5},{5... | collective-permute-start | bytes 12296 | tf_op jit(solution)/shard_map/ppermute | solution.py:62
  102.2 4.0 %collective-permute-start.4 = (f32[8,128]{1,0:T(8,128)S(1)}, f32[8,128]{1,0:T(8,128)S(1)}, u32[]{:S(2)}, u32[]{:S(2)}) collective-permute-start(f32[8,128]{1,0:T(8,128)S(1)} %bitcast_add_fusion.12), channel_id=1, source_target_pairs={{0,8},{4,12},{8,0},{12,4},{16,24},{20,28},{24,16},{28,20},{1,9},{5... | collective-permute-start | bytes 12296 | tf_op jit(solution)/shard_map/ppermute | solution.py:62
  106.3 5.6 %collective-permute-start.5 = (f32[8,128]{1,0:T(8,128)S(1)}, f32[8,128]{1,0:T(8,128)S(1)}, u32[]{:S(2)}, u32[]{:S(2)}) collective-permute-start(f32[8,128]{1,0:T(8,128)S(1)} %fusion.132), channel_id=1, source_target_pairs={{0,16},{4,20},{8,24},{12,28},{16,0},{20,4},{24,8},{28,12},{1,17},{... | collective-permute-start | bytes 12296 | tf_op jit(solution)/shard_map/ppermute | solution.py:62
  114.4 6.6 %collective-permute-start.6 = (bf16[2,1024,384]{2,1,0:T(8,128)(2,1)S(1)}, bf16[2,1024,384]{2,1,0:T(8,128)(2,1)S(1)}, u32[]{:S(2)}, u32[]{:S(2)}) collective-permute-start(bf16[2,1024,384]{2,1,0:T(8,128)(2,1)S(1)} %pad_maximum_fusion), channel_id=1, source_target_pairs={{0,1},{1,0},{2,3},{3,2},{4,5},{5,4},{6,7},{7,6},{8,9},{9,8},{10,11... | collective-permute-start | bytes 4718600 | tf_op jit(solution)/shard_map/ppermute | solution.py:62
  115.7 3.7 %collective-permute-start.8 = (bf16[2,1024,256]{2,1,0:T(8,128)(2,1)S(1)}, bf16[2,1024,256]{2,1,0:T(8,128)(2,1)S(1)}, u32[]{:S(2)}, u32[]{:S(2)}) collective-permute-start(bf16[2,1024,256]{2,1,0:T(8,128)(2,1)S(1)} %pad_maximum_fusion.2), channel_id=1, source_target_pairs={{0,1},{1,0},{2,3},{3,2},{4,5},{5,4},{6,7},{7,6},{8,9},{9,8},{10,11... | collective-permute-start | bytes 3145736 | tf_op jit(solution)/shard_map/ppermute | solution.py:62
  116.8 4.8 %collective-permute-start.7 = (bf16[2,1024,384]{2,1,0:T(8,128)(2,1)S(1)}, bf16[2,1024,384]{2,1,0:T(8,128)(2,1)S(1)}, u32[]{:S(2)}, u32[]{:S(2)}) collective-permute-start(bf16[2,1024,384]{2,1,0:T(8,128)(2,1)S(1)} %pad_maximum_fusion.1), channel_id=1, source_target_pairs={{0,1},{1,0},{2,3},{3,2},{4,5},{5,4},{6,7},{7,6},{8,9},{9,8},{10,11... | collective-permute-start | bytes 4718600 | tf_op jit(solution)/shard_map/ppermute | solution.py:62
  119.6 1.4 copy-start.6
  121.3 1.6 copy-start.1
  123.0 1.7 copy-start.3
  125.6 20.0 %collective-permute-start.9 = (bf16[2,2,2,128,384]{4,3,0,1,2:T(8,128)(2,1)S(1)}, bf16[2,2,2,128,384]{4,3,0,1,2:T(8,128)(2,1)}, u32[]{:S(2)}, u32[]{:S(2)}) collective-permute-start(bf16[2,2,2,128,384]{4,3,0,1,2:T(8,128)(2,1)S(1)} %fusion.30), channel_id=1, source_target_pairs={{0,2},{1,3},{2,0},{3,1},{4,6},{5,7},{6,4},{7,5},{8,10},{9,11},{10,... | collective-permute-start | bytes 2359304 | tf_op jit(solution)/shard_map/ppermute | solution.py:62
  127.1 19.9 %collective-permute-start.10 = (bf16[2,2,2,128,384]{4,3,0,1,2:T(8,128)(2,1)}, bf16[2,2,2,128,384]{4,3,0,1,2:T(8,128)(2,1)}, u32[]{:S(2)}, u32[]{:S(2)}) collective-permute-start(bf16[2,2,2,128,384]{4,3,0,1,2:T(8,128)(2,1)} %fusion.31), channel_id=1, source_target_pairs={{0,4},{4,0},{8,12},{12,8},{16,20},{20,16},{24,28},{28,24},{1,5},{5... | collective-permute-start | bytes 2359304 | tf_op jit(solution)/shard_map/ppermute | solution.py:62
  128.5 13.8 %collective-permute-start.11 = (bf16[2,2,2,128,256]{4,3,2,0,1:T(8,128)(2,1)S(1)}, bf16[2,2,2,128,256]{4,3,2,0,1:T(8,128)(2,1)}, u32[]{:S(2)}, u32[]{:S(2)}) collective-permute-start(bf16[2,2,2,128,256]{4,3,2,0,1:T(8,128)(2,1)S(1)} %fusion.32), channel_id=1, source_target_pairs={{0,8},{4,12},{8,0},{12,4},{16,24},{20,28},{24,16},{28,20},{1,9},{5... | collective-permute-start | bytes 1572872 | tf_op jit(solution)/shard_map/ppermute | solution.py:62
  129.6 22.0 %copy-start.4 = (f32[2,1024,384]{2,1,0:T(8,128)S(1)}, f32[2,1024,384]{2,1,0:T(8,128)}, u32[]{:S(2)}) copy-start(f32[2,1024,384]{2,1,0:T(8,128)} %copy-done.3) | copy-start | bytes 9437188
  148.6 14.5 %collective-permute-start.18 = (bf16[2,2,128,256]{3,2,1,0:T(8,128)(2,1)S(1)}, bf16[2,2,128,256]{3,2,1,0:T(8,128)(2,1)S(1)}, u32[]{:S(2)}, u32[]{:S(2)}) collective-permute-start(bf16[2,2,128,256]{3,2,1,0:T(8,128)(2,1)S(1)} %fusion.44), channel_id=1, source_target_pairs={{0,16},{4,20},{8,24},{12,28},{16,0},{20,4},{24,8},{28,12},{1,17},{... | collective-permute-start | bytes 786440 | tf_op jit(solution)/shard_map/ppermute | solution.py:62
  151.6 12.2 %copy-start.2 = (f32[2,1024,384]{2,1,0:T(8,128)S(1)}, f32[2,1024,384]{2,1,0:T(8,128)}, u32[]{:S(2)}) copy-start(f32[2,1024,384]{2,1,0:T(8,128)} %copy-done.1) | copy-start | bytes 9437188
  153.1 16.7 %collective-permute-start.15 = (bf16[2,2,128,384]{3,2,0,1:T(8,128)(2,1)S(1)}, bf16[2,2,128,384]{3,2,0,1:T(8,128)(2,1)S(1)}, u32[]{:S(2)}, u32[]{:S(2)}) collective-permute-start(bf16[2,2,128,384]{3,2,0,1:T(8,128)(2,1)S(1)} %fusion.43), channel_id=1, source_target_pairs={{0,8},{4,12},{8,0},{12,4},{16,24},{20,28},{24,16},{28,20},{1,9},{5... | collective-permute-start | bytes 1179656 | tf_op jit(solution)/shard_map/ppermute | solution.py:62
  163.2 5.0 %collective-permute-start.19 = (bf16[2,128,256]{2,1,0:T(8,128)(2,1)S(1)}, bf16[2,128,256]{2,1,0:T(8,128)(2,1)S(1)}, u32[]{:S(2)}, u32[]{:S(2)}) collective-permute-start(bf16[2,128,256]{2,1,0:T(8,128)(2,1)S(1)} %fusion.70), channel_id=1, source_target_pairs={{0,2},{1,3},{2,0},{3,1},{4,6},{5,7},{6,4},{7,5},{8,10},{9,11},{10,... | collective-permute-start | bytes 393224 | tf_op jit(solution)/shard_map/ppermute | solution.py:62
  165.2 10.9 %collective-permute-start.12 = (bf16[2,2,128,384]{3,2,0,1:T(8,128)(2,1)S(1)}, bf16[2,2,128,384]{3,2,0,1:T(8,128)(2,1)S(1)}, u32[]{:S(2)}, u32[]{:S(2)}) collective-permute-start(bf16[2,2,128,384]{3,2,0,1:T(8,128)(2,1)S(1)} %fusion.42), channel_id=1, source_target_pairs={{0,4},{4,0},{8,12},{12,8},{16,20},{20,16},{24,28},{28,24},{1,5},{5... | collective-permute-start | bytes 1179656 | tf_op jit(solution)/shard_map/ppermute | solution.py:62
  168.3 9.3 %collective-permute-start.20 = (bf16[128,256]{1,0:T(8,128)(2,1)S(1)}, bf16[128,256]{1,0:T(8,128)(2,1)S(1)}, u32[]{:S(2)}, u32[]{:S(2)}) collective-permute-start(bf16[128,256]{1,0:T(8,128)(2,1)S(1)} %fusion.90), channel_id=1, source_target_pairs={{0,4},{4,0},{8,12},{12,8},{16,20},{20,16},{24,28},{28,24},{1,5},{5... | collective-permute-start | bytes 196616 | tf_op jit(solution)/shard_map/ppermute | solution.py:62
  170.0 10.6 %collective-permute-start.16 = (bf16[2,128,384]{2,1,0:T(8,128)(2,1)S(1)}, bf16[2,128,384]{2,1,0:T(8,128)(2,1)S(1)}, u32[]{:S(2)}, u32[]{:S(2)}) collective-permute-start(bf16[2,128,384]{2,1,0:T(8,128)(2,1)S(1)} %fusion.51), channel_id=1, source_target_pairs={{0,16},{4,20},{8,24},{12,28},{16,0},{20,4},{24,8},{28,12},{1,17},{... | collective-permute-start | bytes 589832 | tf_op jit(solution)/shard_map/ppermute | solution.py:62
  176.2 8.4 %collective-permute-start.13 = (bf16[2,128,384]{2,1,0:T(8,128)(2,1)S(1)}, bf16[2,128,384]{2,1,0:T(8,128)(2,1)S(1)}, u32[]{:S(2)}, u32[]{:S(2)}) collective-permute-start(bf16[2,128,384]{2,1,0:T(8,128)(2,1)S(1)} %fusion.50), channel_id=1, source_target_pairs={{0,8},{4,12},{8,0},{12,4},{16,24},{20,28},{24,16},{28,20},{1,9},{5... | collective-permute-start | bytes 589832 | tf_op jit(solution)/shard_map/ppermute | solution.py:62
  180.7 4.7 %collective-permute-start.17 = (bf16[128,384]{1,0:T(8,128)(2,1)S(1)}, bf16[128,384]{1,0:T(8,128)(2,1)S(1)}, u32[]{:S(2)}, u32[]{:S(2)}) collective-permute-start(bf16[128,384]{1,0:T(8,128)(2,1)S(1)} %fusion.89), channel_id=1, source_target_pairs={{0,2},{1,3},{2,0},{3,1},{4,6},{5,7},{6,4},{7,5},{8,10},{9,11},{10,... | collective-permute-start | bytes 294920 | tf_op jit(solution)/shard_map/ppermute | solution.py:62
  184.6 6.6 %collective-permute-start.14 = (bf16[128,384]{1,0:T(8,128)(2,1)S(1)}, bf16[128,384]{1,0:T(8,128)(2,1)S(1)}, u32[]{:S(2)}, u32[]{:S(2)}) collective-permute-start(bf16[128,384]{1,0:T(8,128)(2,1)S(1)} %fusion.88), channel_id=1, source_target_pairs={{0,16},{4,20},{8,24},{12,28},{16,0},{20,4},{24,8},{28,12},{1,17},{... | collective-permute-start | bytes 294920 | tf_op jit(solution)/shard_map/ppermute | solution.py:62
